TPU v7x, 128 devices: a whole 4x4x4 slice. The times are simulated.
128 devices in a mesh: partner: 16 (over y, x_lo, core), blk: 8 (over z, x_hi).
Axes of the slice: x: 4 (x_hi: 2, x_lo: 2; x = x_hi * 2 + x_lo), y: 4, z: 4, core: 2. Of those that a mesh axis runs over, the one named last changes fastest.
Arguments:
- tensor_slab: float32 [8, 8192, 4096], P(None, 'partner', 'blk'), may hold values from -6 to 6
- sign_flips: int32 [8192], P('partner'), may hold values from -1 to 1, as said below
- mode2_factor: float32 [4096, 64], P('blk'), may hold values from -6 to 6
- mode3_factor: float32 [8, 64], replicated, may hold values from -6 to 6
- fibre_col: int32 [4096], P('blk'), may hold values from 0 to 511
- fibre_depth: int32 [4096], P('blk'), may hold values from 0 to 7
Outputs:
- mixed_slab: float32 [8, 8192, 4096], P(None, 'partner', 'blk')
- factor_update: float32 [8192, 64], P('partner')
Inputs may be any that keep to these rules, and one draw needn't show every extreme that they name: `sign_flips`: every entry is -1 or 1.
All inputs are finite; a program needn't handle non-finite values.
Results may differ from a plain program's by a relative error of at most 0.000098.
Values sent between devices are 32-bit elements; how exact they have to be, the bound alone decides.
No kernel may reach another device: no remote copies, remote signals or barrier semaphores. Data moves between devices by JAX's collectives and lax.ppermute only.
A program may use at most 128 MiB of HBM per device.

v0:
```python
import math

import jax
import jax.numpy as jnp
from jax import lax
from jax.sharding import PartitionSpec as P

ridge = 0.1


def swapped(value, axis, stride):
    mask = 2**stride
    pairs = [(source, source ^ mask) for source in range(lax.axis_size(axis))]
    return lax.ppermute(value, axis, pairs)


def hadamard_table(order_len):
    rows_idx = lax.broadcasted_iota(jnp.int32, (order_len, order_len), 0)
    cols_idx = lax.broadcasted_iota(jnp.int32, (order_len, order_len), 1)
    common = jnp.bitwise_and(rows_idx, cols_idx)
    parity = jnp.zeros((order_len, order_len), jnp.int32)
    for bit_place in range(order_len.bit_length() - 1):
        parity = parity + jnp.bitwise_and(jnp.right_shift(common, bit_place), 1)
    return (1 - 2 * jnp.bitwise_and(parity, 1)).astype(jnp.float32)


def solve_normal(gram, moment):
    factor_chol = jnp.linalg.cholesky(gram)
    return jax.scipy.linalg.cho_solve((factor_chol, True), moment.T).T


def contract_samples(picked, khatri):
    return lax.dot_general(
        picked, khatri, (((0,), (0,)), ((), ())), precision=lax.Precision.HIGHEST
    )


def shards(tensor_slab, sign_flips, mode2_factor, mode3_factor, fibre_col, fibre_depth):
    flipped = tensor_slab * sign_flips.astype(jnp.float32)[None, :, None]
    depth_count, local_rows, block_cols = flipped.shape
    parties = lax.axis_size("partner")
    mixed = jnp.einsum(
        "ab,kbj->kaj", hadamard_table(local_rows), flipped, precision=lax.Precision.HIGHEST
    )
    my_index = lax.axis_index("partner")
    for bit_place in range(parties.bit_length() - 1):
        other_half = swapped(mixed, "partner", bit_place)
        upper_side = jnp.bitwise_and(jnp.right_shift(my_index, bit_place), 1) == 1
        mixed = jnp.where(upper_side, other_half - mixed, mixed + other_half)
    mixed_slab = mixed * (1.0 / math.sqrt(local_rows * parties))
    total_count = fibre_col.shape[0] * lax.axis_size("blk")
    picked = mixed_slab[fibre_depth, :, fibre_col]
    khatri = mode2_factor[fibre_col] * mode3_factor[fibre_depth]
    moment_scale = 1.0 / math.sqrt(total_count)
    gram_part = contract_samples(khatri, khatri) * (1.0 / total_count)
    identity = jnp.eye(khatri.shape[1], dtype=jnp.float32)
    moment_part = contract_samples(picked, khatri) * moment_scale
    moment, gram = lax.psum((moment_part, gram_part), "blk")
    factor_update = solve_normal(gram + ridge * identity, moment)
    return (mixed_slab, factor_update)


def solution(mesh):
    return jax.shard_map(
        shards,
        mesh=mesh,
        in_specs=(P(None, "partner", "blk"), P("partner"), P("blk", None), P(), P("blk"), P("blk")),
        out_specs=(P(None, "partner", "blk"), P("partner", None)),
        check_vma=False,
    )
```

profile of v0, /device:TPU:0, one launch (start us, length us, event | category | flops | bytes accessed | tf_op | source)
XLA Modules:
  0.0 750.9 jit_solution(4079253023349012948)
XLA Ops:
  7.2 0.7 convert_element_type.7
  7.9 33.1 %fusion.3 = f32[8,512,512]{1,2,0:T(8,128)} fusion(f32[8,512,512]{2,1,0:T(8,128)} %param.6, f32[512]{0:T(512)S(1)} %convert_element_type.7), kind=kOutput, calls=%fused_computation.10 | convolution fusion | flops 12895125504 | bytes 16779264 | tf_op jit(solution)/shard_map/ab,kbj->kaj/dot_general | solution.py:42
  41.0 13.5 %collective-permute-done = f32[8,512,512]{1,2,0:T(8,128)} collective-permute-done((f32[8,512,512]{1,2,0:T(8,128)}, f32[8,512,512]{1,2,0:T(8,128)}, u32[]{:S(2)}, u32[]{:S(2)}) %collective-permute-start) | collective-permute-done | bytes 8388640 | tf_op jit(solution)/shard_map/ppermute | solution.py:14
  54.5 11.3 %add_select_fusion.2 = f32[8,512,512]{1,2,0:T(8,128)} fusion(f32[8,512,512]{1,2,0:T(8,128)} %fusion.3, f32[8,512,512]{1,2,0:T(8,128)} %collective-permute-done, pred[]{:T(512)S(6)} %eq.16), kind=kLoop, calls=%fused_computation.6 | loop fusion | flops 6291456 | bytes 25165824 | tf_op jit(solution)/shard_map/jit(_where)/select_n | solution.py:49
  65.8 1.6 collective-permute-start.1
  67.4 181.2 %collective-permute-done.1 = f32[8,512,512]{1,2,0:T(8,128)} collective-permute-done((f32[8,512,512]{1,2,0:T(8,128)}, f32[8,512,512]{1,2,0:T(8,128)}, u32[]{:S(2)}, u32[]{:S(2)}) %collective-permute-start.1) | collective-permute-done | bytes 8388640 | tf_op jit(solution)/shard_map/ppermute | solution.py:14
  248.6 11.3 %add_select_fusion.1 = f32[8,512,512]{1,2,0:T(8,128)} fusion(f32[8,512,512]{1,2,0:T(8,128)} %add_select_fusion.2, f32[8,512,512]{1,2,0:T(8,128)} %collective-permute-done.1, pred[]{:T(512)S(6)} %eq.15), kind=kLoop, calls=%fused_computation.5 | loop fusion | flops 6291456 | bytes 25165824 | tf_op jit(solution)/shard_map/jit(_where)/select_n | solution.py:49
  259.9 1.7 collective-permute-start.2
  261.6 180.3 %collective-permute-done.2 = f32[8,512,512]{1,2,0:T(8,128)} collective-permute-done((f32[8,512,512]{1,2,0:T(8,128)}, f32[8,512,512]{1,2,0:T(8,128)}, u32[]{:S(2)}, u32[]{:S(2)}) %collective-permute-start.2) | collective-permute-done | bytes 8388640 | tf_op jit(solution)/shard_map/ppermute | solution.py:14
  441.9 11.3 %add_select_fusion = f32[8,512,512]{1,2,0:T(8,128)} fusion(f32[8,512,512]{1,2,0:T(8,128)} %add_select_fusion.1, f32[8,512,512]{1,2,0:T(8,128)} %collective-permute-done.2, pred[]{:T(512)S(6)} %eq.14), kind=kLoop, calls=%fused_computation.4 | loop fusion | flops 6291456 | bytes 25165824 | tf_op jit(solution)/shard_map/jit(_where)/select_n | solution.py:49
  453.2 3.3 collective-permute-start.3
  456.7 1.0 gather_fusion
  457.7 1.0 gather_fusion.1
  459.4 43.2 %psum.14 = f32[64,64]{1,0:T(8,128)S(1)} all-reduce(f32[64,64]{1,0:T(8,128)S(1)} %convolution_multiply_fusion.1), channel_id=1, replica_groups=mesh['partner'=16,'blk'=8] {'blk'}, use_global_device_ids=true, to_apply=%region_0.1 | all-reduce | flops 4096 | bytes 32768 | tf_op jit(solution)/shard_map/psum | solution.py:58
  502.7 5.8 cholesky.16
  509.2 126.6 %collective-permute-done.3 = f32[8,512,512]{1,2,0:T(8,128)} collective-permute-done((f32[8,512,512]{1,2,0:T(8,128)}, f32[8,512,512]{1,2,0:T(8,128)}, u32[]{:S(2)}, u32[]{:S(2)}) %collective-permute-start.3) | collective-permute-done | bytes 8388640 | tf_op jit(solution)/shard_map/ppermute | solution.py:14
  635.8 9.5 %select_multiply_fusion = f32[8,512,512]{1,2,0:T(8,128)} fusion(f32[8,512,512]{1,2,0:T(8,128)} %add_select_fusion, f32[8,512,512]{1,2,0:T(8,128)} %collective-permute-done.3, pred[]{:T(512)S(6)} %eq.13), kind=kLoop, calls=%fused_computation.3 | loop fusion | flops 8388608 | bytes 25165824 | tf_op jit(solution)/shard_map/mul | solution.py:50
  645.3 6.6 gather_fusion.2
  651.9 2.5 convolution_multiply_fusion
  655.2 4.9 custom-call.10
  660.1 9.1 %copy.11 = f32[8,512,512]{2,1,0:T(8,128)} copy(f32[8,512,512]{1,2,0:T(8,128)} %select_multiply_fusion) | data formatting | bytes 16777216
  669.2 72.6 %all-reduce.2.cloned.1.call-done = f32[512,64]{1,0:T(8,128)} async-done(((f32[512,64]{1,0:T(8,128)}), f32[512,64]{1,0:T(8,128)}) %all-reduce.2.cloned.1.call-update) | async-done | bytes 131088 | tf_op jit(solution)/shard_map/psum | solution.py:58
  741.8 1.4 fusion.54
  743.2 0.9 fusion.52
  (21 shorter events, 2.2 us)
Async XLA Ops:
  7.2 450.5 %copy-start = (f32[8,64]{1,0:T(8,128)S(1)}, f32[8,64]{1,0:T(8,128)}, u32[]{:S(2)}) copy-start(f32[8,64]{1,0:T(8,128)} %param.9) | copy-start | bytes 6148
  7.2 734.6 %all-reduce.2.cloned.1.call-start = ((), (), s32[]{:S(2)}) async-start(), calls=%async_computation | async-start | bytes 524288 | tf_op jit(solution)/shard_map/psum | solution.py:58
  41.0 13.5 %collective-permute-start = (f32[8,512,512]{1,2,0:T(8,128)}, f32[8,512,512]{1,2,0:T(8,128)}, u32[]{:S(2)}, u32[]{:S(2)}) collective-permute-start(f32[8,512,512]{1,2,0:T(8,128)} %fusion.3), channel_id=1, source_target_pairs={{0,8},{8,0},{16,24},{24,16},{32,40},{40,32},{48,56},{56,48},{64,72... | collective-permute-start | bytes 25165832 | tf_op jit(solution)/shard_map/ppermute | solution.py:14
  65.8 182.8 %collective-permute-start.1 = (f32[8,512,512]{1,2,0:T(8,128)}, f32[8,512,512]{1,2,0:T(8,128)}, u32[]{:S(2)}, u32[]{:S(2)}) collective-permute-start(f32[8,512,512]{1,2,0:T(8,128)} %add_select_fusion.2), channel_id=1, source_target_pairs={{0,16},{8,24},{16,0},{24,8},{32,48},{40,56},{48,32},{56,40},{64,80... | collective-permute-start | bytes 25165832 | tf_op jit(solution)/shard_map/ppermute | solution.py:14
  259.9 182.0 %collective-permute-start.2 = (f32[8,512,512]{1,2,0:T(8,128)}, f32[8,512,512]{1,2,0:T(8,128)}, u32[]{:S(2)}, u32[]{:S(2)}) collective-permute-start(f32[8,512,512]{1,2,0:T(8,128)} %add_select_fusion.1), channel_id=1, source_target_pairs={{0,32},{8,40},{16,48},{24,56},{32,0},{40,8},{48,16},{56,24},{64,96... | collective-permute-start | bytes 25165832 | tf_op jit(solution)/shard_map/ppermute | solution.py:14
  261.6 194.9 %copy-start.1 = (f32[512,64]{0,1:T(8,128)S(1)}, f32[512,64]{0,1:T(8,128)}, u32[]{:S(2)}) copy-start(f32[512,64]{0,1:T(8,128)} %param.8) | copy-start | bytes 393220
  261.6 195.0 %copy-start.2 = (s32[512]{0:T(512)S(1)}, s32[512]{0:T(512)}, u32[]{:S(2)}) copy-start(s32[512]{0:T(512)} %param.11) | copy-start | bytes 6148
  261.6 195.0 %copy-start.3 = (s32[512]{0:T(512)S(1)}, s32[512]{0:T(512)}, u32[]{:S(2)}) copy-start(s32[512]{0:T(512)} %param.10) | copy-start | bytes 6148
  453.2 182.6 %collective-permute-start.3 = (f32[8,512,512]{1,2,0:T(8,128)}, f32[8,512,512]{1,2,0:T(8,128)}, u32[]{:S(2)}, u32[]{:S(2)}) collective-permute-start(f32[8,512,512]{1,2,0:T(8,128)} %add_select_fusion), channel_id=1, source_target_pairs={{0,64},{8,72},{16,80},{24,88},{32,96},{40,104},{48,112},{56,120},{... | collective-permute-start | bytes 25165832 | tf_op jit(solution)/shard_map/ppermute | solution.py:14
Sparse Core Ops, SparseCore 0:
  654.6 87.1 all-reduce.1
where the time goes:
time: 751 us
  waiting for transfers between devices  574 us (76%)
  other arithmetic  56.2 us (7%)
  blocking collectives  43.2 us (6%)
  matrix products  38.5 us (5%)
  local copies, waits for them, and re-layouts  18.1 us (2%)
  between operations  14.2 us (2%)
    ppermute x4, waiting for transfers between devices, swapped(): return lax.ppermute(value, axis, pairs)  502 us
    psum x1, waiting for transfers between devices, shards(): moment, gram = lax.psum((moment_part, gram_part), 'blk')  72.6 us
    psum x1, blocking collectives, shards(): moment, gram = lax.psum((moment_part, gram_part), 'blk')  43.2 us
    select_n x3, other arithmetic, shards(): mixed = jnp.where(upper_side, other_half - mixed, mixed + other_half)  33.9 us
    dot_general x1, matrix products, shards(): jnp.einsum('ab,kbj->kaj', hadamard_table(local_rows), flipped, precision=...  33.1 us
  transfers between devices with their start and end apart: 5, of which 5 were waited for; matrix products, arithmetic and copies ran while one was open for 3% of the time, Pallas kernels for 0%

commit v1 on v0

v1 whole, which is shorter than its diff:
```python
import functools
import math

import jax
import jax.numpy as jnp
import numpy as np
from jax import lax
from jax.experimental import pallas as pl
from jax.experimental.pallas import tpu as pltpu
from jax.sharding import PartitionSpec as P

ridge = 0.1
HIGH = lax.Precision.HIGHEST


def hadamard(order_len):
    table = np.ones((1, 1), np.float32)
    while table.shape[0] < order_len:
        table = np.block([[table, table], [table, -table]])
    return table


def butterflies(parts):
    stride = 1
    while stride < len(parts):
        parts = [
            parts[i] + parts[i + stride] if not i & stride else parts[i - stride] - parts[i]
            for i in range(len(parts))
        ]
        stride *= 2
    return parts


def middle_kernel(signs_ref, table_ref, x_ref, o_ref):
    table = table_ref[...]
    flipped = [x_ref[p] * signs_ref[p] for p in range(x_ref.shape[0])]
    for p, value in enumerate(butterflies(flipped)):
        high = value.astype(jnp.bfloat16)
        low = (value - high.astype(jnp.float32)).astype(jnp.bfloat16)
        o_ref[p] = jnp.dot(table, high, preferred_element_type=jnp.float32) + jnp.dot(
            table, low, preferred_element_type=jnp.float32
        )


def middle(signs, table, x, tile):
    parties, rows, cols = x.shape
    return pl.pallas_call(
        middle_kernel,
        out_shape=jax.ShapeDtypeStruct(x.shape, jnp.float32),
        grid=(cols // tile,),
        in_specs=[
            pl.BlockSpec((parties, rows, 1), lambda j: (0, 0, 0)),
            pl.BlockSpec((rows, rows), lambda j: (0, 0)),
            pl.BlockSpec((parties, rows, tile), lambda j: (0, 0, j)),
        ],
        out_specs=pl.BlockSpec((parties, rows, tile), lambda j: (0, 0, j)),
        compiler_params=pltpu.CompilerParams(vmem_limit_bytes=48 * 2**20),
        cost_estimate=pl.CostEstimate(
            flops=4 * parties * rows * rows * cols, bytes_accessed=8 * x.size, transcendentals=0
        ),
    )(signs, table, x)


def end_kernel(scale, x_ref, o_ref):
    half = x_ref.shape[1] // 2
    upper, lower = x_ref[0, :half] * scale, x_ref[0, half:] * scale
    o_ref[0, :half] = upper + lower
    o_ref[0, half:] = upper - lower


def end(x, scale):
    depth, rows, cols = x.shape
    block = pl.BlockSpec((1, rows, cols), lambda k: (k, 0, 0))
    return pl.pallas_call(
        functools.partial(end_kernel, scale),
        out_shape=jax.ShapeDtypeStruct(x.shape, jnp.float32),
        grid=(depth,),
        in_specs=[block],
        out_specs=block,
        compiler_params=pltpu.CompilerParams(vmem_limit_bytes=32 * 2**20),
        cost_estimate=pl.CostEstimate(flops=3 * x.size, bytes_accessed=8 * x.size, transcendentals=0),
    )(x)


def sample_kernel(col_ref, depth_ref, signs_ref, mode2_ref, mode3_ref, x_ref, o_ref):
    k = pl.program_id(0)
    rows, cols = x_ref.shape[1:]
    chosen = jnp.where(depth_ref[...] == k, col_ref[...], -1)
    hits = lax.broadcasted_iota(jnp.int32, (cols, chosen.shape[1]), 0) == chosen
    count = jnp.sum(hits.astype(jnp.float32), axis=1, keepdims=True)
    khatri = mode2_ref[...] * mode3_ref[0]
    weighted = khatri * count

    @pl.when(k == 0)
    def _():
        o_ref[...] = jnp.zeros_like(o_ref)

    o_ref[:rows] += signs_ref[...] * jnp.dot(
        x_ref[0], weighted, precision=HIGH, preferred_element_type=jnp.float32
    )
    o_ref[rows:] += lax.dot_general(
        khatri, weighted, (((0,), (0,)), ((), ())), precision=HIGH, preferred_element_type=jnp.float32
    )


def sample(col, depth, signs, mode2, mode3, x):
    slices, rows, cols = x.shape
    rank = mode2.shape[1]
    whole = lambda *shape: pl.BlockSpec(shape, lambda k: (0,) * len(shape))
    return pl.pallas_call(
        sample_kernel,
        out_shape=jax.ShapeDtypeStruct((rows + rank, rank), jnp.float32),
        grid=(slices,),
        in_specs=[
            whole(1, col.shape[0]),
            whole(1, col.shape[0]),
            whole(rows, 1),
            whole(cols, rank),
            pl.BlockSpec((1, 1, rank), lambda k: (k, 0, 0)),
            pl.BlockSpec((1, rows, cols), lambda k: (k, 0, 0)),
        ],
        out_specs=whole(rows + rank, rank),
        compiler_params=pltpu.CompilerParams(vmem_limit_bytes=32 * 2**20),
        cost_estimate=pl.CostEstimate(
            flops=12 * x.size * rank, bytes_accessed=4 * x.size, transcendentals=0
        ),
    )(col[None], depth[None], signs[:, None], mode2, mode3[:, None], x)


def solve_normal(gram, moment):
    factor_chol = jnp.linalg.cholesky(gram)
    return jax.scipy.linalg.cho_solve((factor_chol, True), moment.T).T


def shards(tensor_slab, sign_flips, mode2_factor, mode3_factor, fibre_col, fibre_depth):
    slices, rows, cols = tensor_slab.shape
    parties = lax.axis_size("partner")
    me = lax.axis_index("partner")
    rank = mode2_factor.shape[1]
    total = fibre_col.shape[0] * lax.axis_size("blk")
    signs = sign_flips.astype(jnp.float32)
    piece = slices * rows // parties
    halves = rows // piece

    sent = lax.all_to_all(tensor_slab.reshape(parties, piece, cols), "partner", 0, 0)
    all_signs = lax.all_gather(signs, "partner").reshape(parties, halves, piece)
    my_signs = lax.dynamic_index_in_dim(all_signs, me % halves, 1, keepdims=False)
    table = jnp.asarray(hadamard(piece), jnp.bfloat16)
    mixed = middle(my_signs[..., None], table, sent, 128)
    back = lax.all_to_all(mixed, "partner", 0, 0).reshape(slices, rows, cols)
    mixed_slab = end(back, 1.0 / math.sqrt(rows * parties))

    part = sample(fibre_col, fibre_depth, signs, mode2_factor, mode3_factor, tensor_slab)
    summed = lax.psum(part, "blk")
    gram = summed[rows:] * (1.0 / total) + ridge * jnp.eye(rank, dtype=jnp.float32)
    solved = solve_normal(gram, summed[:rows])
    scale = 1.0 / math.sqrt(total) / math.sqrt(rows * parties)
    factor = jnp.dot(jnp.asarray(hadamard(rows)), solved, precision=HIGH) * scale
    for bit in range(parties.bit_length() - 1):
        other = lax.ppermute(factor, "partner", [(s, s ^ (1 << bit)) for s in range(parties)])
        upper = jnp.bitwise_and(jnp.right_shift(me, bit), 1) == 1
        factor = jnp.where(upper, other - factor, factor + other)
    return (mixed_slab, factor)


def solution(mesh):
    return jax.shard_map(
        shards,
        mesh=mesh,
        in_specs=(P(None, "partner", "blk"), P("partner"), P("blk", None), P(), P("blk"), P("blk")),
        out_specs=(P(None, "partner", "blk"), P("partner", None)),
        check_vma=False,
    )
```

time: 751 us -> 295 us (0.39)
  waiting for transfers between devices: 574 us -> 105 us
  blocking collectives: 43.2 us -> 107 us
  other arithmetic: 56.2 us -> 14.4 us
  matrix products: 38.5 us -> 2.77 us
  Pallas kernels: 0 us -> 31.1 us
  local copies, waits for them, and re-layouts: 18.1 us -> 4.42 us
  starting transfers between devices: 6.55 us -> 15.5 us
    ppermute x4, waiting for transfers between devices: 502 us -> 13.9 us  [shards(): lax.ppermute(factor, 'partner', [(s, s ^ 1 << bit) for s in range(parties)])]
    all_gather x0 -> x1, blocking collectives: none -> 107 us  [shards(): all_signs = lax.all_gather(signs, 'partner').reshape(parties, halves, piece)]
    psum x1 -> x0, blocking collectives: 43.2 us -> none  [shards(): moment, gram = lax.psum((moment_part, gram_part), 'blk')]
    dot_general x3 -> x1, matrix products: 36.2 us -> 1.12 us  [shards(): jnp.dot(jnp.asarray(hadamard(rows)), solved, precision=HIGH) * scale]
    select_n x4, other arithmetic: 33.9 us -> 0.73 us  [shards(): factor = jnp.where(upper, other - factor, factor + other)]
    pallas_call x0 -> x3, Pallas kernels: none -> 31.1 us  [the longest x1 11.1 us: sample(): pl.pallas_call(sample_kernel, out_shape=jax.ShapeDtypeStruct((rows + rank...]
    psum x1, waiting for transfers between devices: 72.6 us -> 91.5 us  [shards(): summed = lax.psum(part, 'blk')]
    all_to_all x0 -> x2, starting transfers between devices: none -> 10.7 us  [the longest x1 5.78 us: shards(): lax.all_to_all(tensor_slab.reshape(parties, piece, cols), 'partner', 0, 0)]
  transfers between devices with their start and end apart: 5 -> 7, of which waited for: 5 -> 5; matrix products, arithmetic and copies ran while one was open for 3% -> 6% of each run, Pallas kernels for 0% -> 4%
where the time goes in v1:
time: 295 us; the launch traced here: 294 us
  blocking collectives  107 us (36%)
  waiting for transfers between devices  105 us (36%)
  Pallas kernels  31.1 us (11%)
  starting transfers between devices  15.5 us (5%)
  other arithmetic  14.4 us (5%)
  between operations  14.3 us (5%)
  local copies, waits for them, and re-layouts  4.42 us (1%)
    all_gather x1, blocking collectives, shards(): all_signs = lax.all_gather(signs, 'partner').reshape(parties, halves, piece)  107 us
    psum x1, waiting for transfers between devices, shards(): summed = lax.psum(part, 'blk')  91.5 us
    ppermute x4, waiting for transfers between devices, shards(): lax.ppermute(factor, 'partner', [(s, s ^ 1 << bit) for s in range(parties)])  13.9 us
    pallas_call x1, Pallas kernels, sample(): pl.pallas_call(sample_kernel, out_shape=jax.ShapeDtypeStruct((rows + rank...  11.1 us
    pallas_call x1, Pallas kernels, middle(): pl.pallas_call(middle_kernel, out_shape=jax.ShapeDtypeStruct(x.shape, jnp...  11 us
    pallas_call x1, Pallas kernels, end(): pl.pallas_call(functools.partial(end_kernel, scale), out_shape=jax.ShapeD...  9.08 us
    another operation x3, other arithmetic, solve_normal(): factor_chol = jnp.linalg.cholesky(gram)  6.52 us
  transfers between devices with their start and end apart: 7, of which 5 were waited for; matrix products, arithmetic and copies ran while one was open for 6% of the time, Pallas kernels for 4%

profile of v1, /device:TPU:0, one launch (start us, length us, event | category | flops | bytes accessed | tf_op | source)
XLA Modules:
  0.0 294.5 jit_solution(12178848187478551527)
XLA Ops:
  7.2 5.8 %all-to-all-start = ((f32[16,256,512]{2,1,0:T(8,128)}), f32[16,256,512]{2,1,0:T(8,128)}, u32[]{:S(2)}, u32[]{:S(2)}) async-start(f32[16,256,512]{2,1,0:T(8,128)} %bitcast.23), calls=%async_computation | async-start | bytes 16777216 | tf_op jit(solution)/shard_map/all_to_all | solution.py:145
  13.0 106.6 %all-gather.1 = f32[16,1,512]{2,1,0:T(1,128)S(1)} all-gather(f32[1,1,512]{2,1,0:T(1,128)S(1)} %bitcast.27), channel_id=2, replica_groups=mesh['partner'=16,'blk'=8] {'partner'}, dimensions={0}, use_global_device_ids=true | all-gather | bytes 34816 | tf_op jit(solution)/shard_map/all_gather | solution.py:146
  119.7 0.6 broadcast_in_dim.22.signs_ref
  120.4 11.0 %shard_map.95 = f32[16,256,512]{2,1,0:T(8,128)} custom-call(f32[16,256,1]{2,1,0:T(8,128)S(1)} %broadcast_in_dim.22.signs_ref, bf16[256,256]{1,0:T(8,128)(2,1)S(1)} %copy-done.1, f32[16,256,512]{2,1,0:T(8,128)} %all-to-all-done.x_ref), custom_call_target="tpu_custom_call" | custom-call | flops 2147483648 | bytes 16777216 | tf_op jit(solution)/shard_map/pallas_call | solution.py:47
  131.4 4.9 %all-to-all-start.1 = ((f32[16,256,512]{2,1,0:T(8,128)}), f32[16,256,512]{2,1,0:T(8,128)}, u32[]{:S(2)}, u32[]{:S(2)}) async-start(f32[16,256,512]{2,1,0:T(8,128)} %shard_map.95), calls=%async_computation.1 | async-start | bytes 16777216 | tf_op jit(solution)/shard_map/all_to_all | solution.py:150
  136.6 3.4 %copy-done = f32[8,512,512]{2,1,0:T(8,128)S(1)} copy-done((f32[8,512,512]{2,1,0:T(8,128)S(1)}, f32[8,512,512]{2,1,0:T(8,128)}, u32[]{:S(2)}) %copy-start) | copy-done | bytes 8388632
  140.0 11.1 %shard_map.97 = f32[576,64]{1,0:T(8,128)} custom-call(s32[1,512]{1,0:T(1,128)S(1)} %bitcast.25, s32[1,512]{1,0:T(1,128)S(1)} %bitcast.26, f32[512,1]{1,0:T(8,128)S(1)} %copy.17.signs_ref, f32[512,64]{1,0:T(8,128)S(1)} %copy.18.mode2_ref, f32[8,1,64]{2,1,0:T(1,128)S(1)} %bitcast.24, f32[8,512,512]{2,1,0:T(8,128)S(1)} %copy-done), custom_call_target="tpu_custom_call" | custom-call | flops 1610612736 | bytes 8388608 | tf_op jit(solution)/shard_map/pallas_call | solution.py:110
  151.1 91.5 %all-reduce.2.cloned.1.call-done = f32[576,64]{1,0:T(8,128)} async-done(((f32[576,64]{1,0:T(8,128)}), f32[576,64]{1,0:T(8,128)}) %all-reduce.2.cloned.1.call-update) | async-done | bytes 147472 | tf_op jit(solution)/shard_map/psum | solution.py:154
  242.6 0.8 fusion.4
  243.5 0.8 fusion.8
  244.3 5.8 %cholesky.16 = f32[64,64]{1,0:T(8,128)S(1)} custom-call(f32[64,64]{1,0:T(8,128)S(1)} %fusion.8), custom_call_target="Cholesky" | custom-call | tf_op jit(solution)/shard_map/jit(cholesky)/cholesky | solution.py:131
  250.1 0.6 compare_reduce_fusion
  250.8 0.7 fusion.3
  251.4 4.9 %custom-call.10 = f32[1,64,64]{1,2,0:T(8,128)S(1)} custom-call(f32[1,64,64]{2,1,0:T(8,128)S(1)} %fusion.3), custom_call_target="InvertDiagBlocksLowerTriangular" | custom-call | tf_op jit(solution)/shard_map/jit(_cho_solve)/triangular_solve | solution.py:132
  256.3 1.4 fusion.1
  258.0 1.1 fusion
  259.2 1.3 collective-permute-done
  260.7 5.5 %collective-permute-done.1 = f32[512,64]{0,1:T(8,128)S(1)} collective-permute-done((f32[512,64]{0,1:T(8,128)S(1)}, f32[512,64]{0,1:T(8,128)S(1)}, u32[]{:S(2)}, u32[]{:S(2)}) %collective-permute-start.1) | collective-permute-done | bytes 131104 | tf_op jit(solution)/shard_map/ppermute | solution.py:160
  266.2 1.5 collective-permute-start.2
  267.8 3.5 %collective-permute-done.2 = f32[512,64]{0,1:T(8,128)S(1)} collective-permute-done((f32[512,64]{0,1:T(8,128)S(1)}, f32[512,64]{0,1:T(8,128)S(1)}, u32[]{:S(2)}, u32[]{:S(2)}) %collective-permute-start.2) | collective-permute-done | bytes 131104 | tf_op jit(solution)/shard_map/ppermute | solution.py:160
  271.3 3.0 %collective-permute-start.3 = (f32[512,64]{0,1:T(8,128)S(1)}, f32[512,64]{0,1:T(8,128)S(1)}, u32[]{:S(2)}, u32[]{:S(2)}) collective-permute-start(f32[512,64]{0,1:T(8,128)S(1)} %add_select_fusion.1), channel_id=1, source_target_pairs={{0,64},{8,72},{16,80},{24,88},{32,96},{40,104},{48,112},{56,120},{... | collective-permute-start | bytes 393224 | tf_op jit(solution)/shard_map/ppermute | solution.py:160
  274.3 3.5 %collective-permute-done.3 = f32[512,64]{0,1:T(8,128)S(1)} collective-permute-done((f32[512,64]{0,1:T(8,128)S(1)}, f32[512,64]{0,1:T(8,128)S(1)}, u32[]{:S(2)}, u32[]{:S(2)}) %collective-permute-start.3) | collective-permute-done | bytes 131104 | tf_op jit(solution)/shard_map/ppermute | solution.py:160
  277.9 0.7 add_select_fusion
  278.5 9.1 %shard_map.96 = f32[8,512,512]{2,1,0:T(8,128)} custom-call(f32[8,512,512]{2,1,0:T(8,128)} %bitcast.2.x_ref), custom_call_target="tpu_custom_call" | custom-call | flops 6291456 | bytes 16777216 | tf_op jit(solution)/shard_map/pallas_call | solution.py:74
  (33 shorter events, 1.1 us)
Async XLA Ops:
  7.2 5.8 %copy-start.7 = (s32[512]{0:T(512)S(1)}, s32[512]{0:T(512)}, u32[]{:S(2)}) copy-start(s32[512]{0:T(512)} %param.9) | copy-start | bytes 6148
  7.2 113.2 %copy-start.1 = (bf16[256,256]{1,0:T(8,128)(2,1)S(1)}, bf16[256,256]{1,0:T(8,128)(2,1)}, u32[]{:S(2)}) copy-start(bf16[256,256]{1,0:T(8,128)(2,1)} %constant.87.clone.table_ref) | copy-start | bytes 393220
  7.2 113.2 %all-to-all-start = ((f32[16,256,512]{2,1,0:T(8,128)}), f32[16,256,512]{2,1,0:T(8,128)}, u32[]{:S(2)}, u32[]{:S(2)}) async-start(f32[16,256,512]{2,1,0:T(8,128)} %bitcast.23), calls=%async_computation | async-start | bytes 16777216 | tf_op jit(solution)/shard_map/all_to_all | solution.py:145
  131.3 5.1 %copy-start.6 = (f32[512,64]{0,1:T(8,128)S(1)}, f32[512,64]{0,1:T(8,128)}, u32[]{:S(2)}) copy-start(f32[512,64]{0,1:T(8,128)} %param.10) | copy-start | bytes 393220
  131.3 5.3 %copy-start.2 = (f32[8,64]{1,0:T(8,128)S(1)}, f32[8,64]{1,0:T(8,128)}, u32[]{:S(2)}) copy-start(f32[8,64]{1,0:T(8,128)} %param.11) | copy-start | bytes 6148
  131.3 5.3 %copy-start.3 = (s32[512]{0:T(512)S(1)}, s32[512]{0:T(512)}, u32[]{:S(2)}) copy-start(s32[512]{0:T(512)} %param.12) | copy-start | bytes 6148
  131.3 5.3 %copy-start.4 = (s32[512]{0:T(512)S(1)}, s32[512]{0:T(512)}, u32[]{:S(2)}) copy-start(s32[512]{0:T(512)} %param.13) | copy-start | bytes 6148
  131.3 126.7 %copy-start.5 = (f32[512,512]{1,0:T(8,128)S(1)}, f32[512,512]{1,0:T(8,128)}, u32[]{:S(2)}) copy-start(f32[512,512]{1,0:T(8,128)} %constant.88.clone) | copy-start | bytes 3145732
  131.4 147.2 %all-to-all-start.1 = ((f32[16,256,512]{2,1,0:T(8,128)}), f32[16,256,512]{2,1,0:T(8,128)}, u32[]{:S(2)}, u32[]{:S(2)}) async-start(f32[16,256,512]{2,1,0:T(8,128)} %shard_map.95), calls=%async_computation.1 | async-start | bytes 16777216 | tf_op jit(solution)/shard_map/all_to_all | solution.py:150
  136.3 106.4 %all-reduce.2.cloned.1.call-start = ((), (), s32[]{:S(2)}) async-start(), calls=%async_computation.2 | async-start | bytes 589824 | tf_op jit(solution)/shard_map/psum | solution.py:154
  136.6 3.4 %copy-start = (f32[8,512,512]{2,1,0:T(8,128)S(1)}, f32[8,512,512]{2,1,0:T(8,128)}, u32[]{:S(2)}) copy-start(f32[8,512,512]{2,1,0:T(8,128)} %x_ref.1) | copy-start | bytes 25165828
  259.1 1.4 collective-permute-start
  260.6 5.6 %collective-permute-start.1 = (f32[512,64]{0,1:T(8,128)S(1)}, f32[512,64]{0,1:T(8,128)S(1)}, u32[]{:S(2)}, u32[]{:S(2)}) collective-permute-start(f32[512,64]{0,1:T(8,128)S(1)} %add_select_fusion.3), channel_id=1, source_target_pairs={{0,16},{8,24},{16,0},{24,8},{32,48},{40,56},{48,32},{56,40},{64,80... | collective-permute-start | bytes 393224 | tf_op jit(solution)/shard_map/ppermute | solution.py:160
  266.2 5.0 %collective-permute-start.2 = (f32[512,64]{0,1:T(8,128)S(1)}, f32[512,64]{0,1:T(8,128)S(1)}, u32[]{:S(2)}, u32[]{:S(2)}) collective-permute-start(f32[512,64]{0,1:T(8,128)S(1)} %add_select_fusion.2), channel_id=1, source_target_pairs={{0,32},{8,40},{16,48},{24,56},{32,0},{40,8},{48,16},{56,24},{64,96... | collective-permute-start | bytes 393224 | tf_op jit(solution)/shard_map/ppermute | solution.py:160
  271.3 6.6 %collective-permute-start.3 = (f32[512,64]{0,1:T(8,128)S(1)}, f32[512,64]{0,1:T(8,128)S(1)}, u32[]{:S(2)}, u32[]{:S(2)}) collective-permute-start(f32[512,64]{0,1:T(8,128)S(1)} %add_select_fusion.1), channel_id=1, source_target_pairs={{0,64},{8,72},{16,80},{24,88},{32,96},{40,104},{48,112},{56,120},{... | collective-permute-start | bytes 393224 | tf_op jit(solution)/shard_map/ppermute | solution.py:160
Sparse Core Ops, SparseCore 0:
  151.2 91.3 all-reduce.1

commit v2 on v0

v2 whole, which is shorter than its diff:
```python
import functools
import math

import jax
import jax.numpy as jnp
import numpy as np
from jax import lax
from jax.experimental import pallas as pl
from jax.experimental.pallas import tpu as pltpu
from jax.sharding import PartitionSpec as P

ridge = 0.1
HIGH = lax.Precision.HIGHEST
F32 = jnp.float32
HBM = pl.BlockSpec(memory_space=pltpu.HBM)
COST = 30_000_000
VMEM = pl.BlockSpec(memory_space=pltpu.VMEM)
SMEM = pl.BlockSpec(memory_space=pltpu.SMEM)


def hadamard(order_len):
    table = np.ones((1, 1), np.float32)
    while table.shape[0] < order_len:
        table = np.block([[table, table], [table, -table]])
    return table


def sign_of(bit):
    return (1 - 2 * bit).astype(F32)


def y_signs(place_ref):
    low, high = sign_of(place_ref[0] & 1), sign_of(place_ref[0] >> 1)
    return [jnp.float32(1), low, high, low * high]


def struct(*shape):
    return jax.ShapeDtypeStruct(shape, F32)


class Chain:
    def __init__(self, place):
        self.place, self.mark = place, None

    def __call__(self, body, operands, in_specs, out_shapes, out_specs, aliases=None, scratch=(), grid=(), limit=12, cost=0):
        marks = () if self.mark is None else (self.mark,)
        n_in, n_out = len(operands), len(out_shapes)

        def inner(place_ref, *refs):
            outs = refs[n_in + len(marks):]
            body(place_ref, *refs[:n_in], *outs[:n_out], *outs[n_out + 1:])

        *outs, self.mark = pl.pallas_call(
            inner,
            out_shape=list(out_shapes) + [struct(8, 128)],
            grid=grid,
            in_specs=[SMEM] + list(in_specs) + [HBM] * len(marks),
            out_specs=list(out_specs) + [HBM],
            scratch_shapes=scratch,
            input_output_aliases=aliases or {},
            compiler_params=pltpu.CompilerParams(vmem_limit_bytes=limit * 2**20),
            cost_estimate=pl.CostEstimate(flops=0, bytes_accessed=cost, transcendentals=0),
        )(self.place, *operands, *marks)
        return outs


def by_rows(rows, step, work):
    def one(i, carry):
        work(pl.ds(pl.multiple_of(i * step, step), step))
        return carry

    lax.fori_loop(0, rows // step, one, 0)


def first(chain, slab, signs, table, groups):
    rows, cols = slab.shape[1:]

    def body(place_ref, signs_ref, table_ref, x_ref, *refs):
        o_refs, held, sems = refs[:2], refs[2], refs[3]
        copies = [
            pltpu.make_async_copy(x_ref.at[2 * group + i], held.at[2 * n + i], sems.at[2 * n + i])
            for n, group in enumerate(groups) for i in range(2)
        ]
        for copy in copies:
            copy.start()
        for n, copy in enumerate(copies):
            copy.wait()
            value = held[n] * signs_ref[...]
            high = value.astype(jnp.bfloat16)
            low = (value - high.astype(F32)).astype(jnp.bfloat16)
            o_refs[n // 2][n % 2] = jnp.dot(table_ref[...], high, preferred_element_type=F32) + jnp.dot(
                table_ref[...], low, preferred_element_type=F32
            )

    return chain(
        body, (signs, table, slab), [VMEM, VMEM, HBM], [struct(2, rows, cols)] * 2, [VMEM] * 2,
        scratch=[pltpu.VMEM((4, rows, cols), F32), pltpu.SemaphoreType.DMA((4,))], limit=48,
    )


def combine_split(chain, which, own, other):
    rows, cols = own.shape[1:]
    half = rows // 2

    def body(place_ref, a_ref, b_ref, *o_refs):
        sign = sign_of(place_ref[which])
        for m in range(4):
            piece = place_ref[0] ^ m
            a, b = (ref.at[piece >> 1, pl.ds(pl.multiple_of((piece & 1) * half, half), half)] for ref in (a_ref, b_ref))

            def work(at, a=a, b=b, o=o_refs[m]):
                o[at, :] = b[at, :] + a[at, :] * sign

            by_rows(half, 64, work)

    return chain(body, (own, other), [VMEM] * 2, [struct(half, cols)] * 4, [VMEM] * 4)


def combine_one(chain, which, own, other, k):
    rows, cols = own.shape[1:]

    def body(place_ref, a_ref, b_ref, o_ref):
        sign = sign_of(place_ref[which])

        def work(at):
            o_ref[at, :] = b_ref[k, at, :] + a_ref[k, at, :] * sign

        by_rows(rows, 64, work)

    return chain(body, (own, other), [VMEM] * 2, [struct(rows, cols)], [VMEM])[0]


def combine_split_slices(chain, which, own, other):
    rows, cols = own[0].shape
    half, extra = rows // 2, (own[1].shape[0] - rows) // 4

    def body(place_ref, *refs):
        sign = sign_of(place_ref[which])
        for m in range(4):
            piece = place_ref[0] ^ m
            for k in range(2):
                @pl.when(piece >> 1 == k)
                def _(m=m, k=k, piece=piece):
                    a, b = (ref.at[pl.ds(pl.multiple_of((piece & 1) * half, half), half)] for ref in (refs[k], refs[2 + k]))

                    def work(at):
                        refs[4 + m][at, :] = b[at, :] + a[at, :] * sign

                    by_rows(half, 64, work)

            if extra:
                at = pl.ds(pl.multiple_of(rows + piece * extra, extra), extra)
                refs[4 + m][half:] = refs[3][at, :] + refs[1][at, :] * sign

    return chain(
        body, tuple(own) + tuple(other), [VMEM] * 4, [struct(half + extra, cols)] * 4, [VMEM] * 4
    )


def middle(chain, parts):
    half, cols = parts[0].shape

    def body(place_ref, *refs):
        signs = y_signs(place_ref)

        def work(at):
            a, b, c, d = (refs[m][at, :] * signs[m] for m in range(4))
            s, t, u, v = a + b, a - b, c + d, c - d
            for m, value in enumerate((s + u, t + v, s - u, t - v)):
                refs[4 + m][at, :] = value * (signs[3] * signs[m])

        by_rows(half, 16, work)

    return chain(body, tuple(parts), [VMEM] * 4, [struct(half, cols)] * 4, [VMEM] * 4)


def pack(chain, parts):
    half, cols = parts[0].shape

    def body(place_ref, *refs):
        for m in range(4):
            def work(at, m=m):
                refs[4 + m // 2][m % 2, at, :] = refs[m][at, :]

            by_rows(half, 64, work)

    return chain(body, tuple(parts), [VMEM] * 4, [struct(2, half, cols)] * 2, [VMEM] * 2)


def gate(chain, values, after):
    n = len(values)

    def body(place_ref, *refs):
        for i in range(n):
            flat = refs[i].shape[0] if len(refs[i].shape) == 2 else None

            def work(at, i=i):
                refs[n + len(after) + i][at] = refs[i][at]

            if flat:
                by_rows(flat, 16, work)
            else:
                by_rows(refs[i].shape[0], 1, work)

    return chain(
        body, tuple(values) + tuple(after), [VMEM] * (n + len(after)), [struct(*v.shape) for v in values], [VMEM] * n
    )


def to_place(place_ref, source, out, group, m, half, sem):
    piece = place_ref[0] ^ m
    start = pl.multiple_of((piece & 1) * half, half)
    copy = pltpu.make_async_copy(source, out.at[2 * group + (piece >> 1), pl.ds(start, half), :], sem)
    copy.start()
    return copy


def end_slices(chain, which, own, other, group, shape):
    half, cols = own[0].shape[1:]

    def body(place_ref, *refs):
        out, held, sems = refs[4:]
        sign = sign_of(place_ref[which])
        copies = []
        for m in range(4):
            def work(at, m=m):
                held[m, at, :] = refs[2 + m // 2][m % 2, at, :] + refs[m // 2][m % 2, at, :] * sign

            by_rows(half, 64, work)
            copies.append(to_place(place_ref, held.at[m], out, group, m, half, sems.at[m]))
        for copy in copies:
            copy.wait()

    return chain(
        body, tuple(own) + tuple(other), [VMEM] * 4, [struct(*shape)], [HBM],
        scratch=[pltpu.VMEM((4, half, cols), F32), pltpu.SemaphoreType.DMA((4,))],
    )[0]


def end_mixed(chain, parts, group, which, own, other, other_group, first_piece, buffer, cost):
    half, cols = buffer.shape[1] // 2, buffer.shape[2]
    names = list(parts)
    n, pieces = len(names), 0 if own is None else own.shape[0]
    pair = () if own is None else (own, other)

    def body(place_ref, *refs):
        out, held, sems = refs[n + len(pair) + 1:]
        copies = [to_place(place_ref, refs[i], out, group, m, half, sems.at[i]) for i, m in enumerate(names)]
        for m in range(pieces):
            def work(at, m=m):
                held[m, at, :] = refs[n + 1][m, at, :] + refs[n][m, at, :] * sign_of(place_ref[which])

            by_rows(half, 64, work)
            copies.append(to_place(place_ref, held.at[m], out, other_group, first_piece + m, half, sems.at[n + m]))
        for copy in copies:
            copy.wait()

    return chain(
        body, tuple(parts[m] for m in names) + pair + (buffer,), [VMEM] * (n + len(pair)) + [HBM],
        [struct(*buffer.shape)], [HBM], aliases={n + len(pair) + 1: 0}, cost=cost,
        scratch=[pltpu.VMEM((max(pieces, 1), half, cols), F32), pltpu.SemaphoreType.DMA((n + pieces,))],
    )[0]


def times_inverse(chain, moment, inverse):
    rank, rows = moment.shape

    def body(place_ref, a_ref, inverse_ref, o_ref):
        o_ref[...] = lax.dot_general(
            a_ref[...], inverse_ref[...], (((0,), (0,)), ((), ())), precision=HIGH, preferred_element_type=F32
        )

    return chain(body, (moment, inverse), [VMEM] * 2, [struct(rows, rank)], [VMEM])[0]


def sample(chain, col, depth, signs, mode2, mode3, slab, table, factor):
    slices, rows, cols = slab.shape
    samples, rank = col.shape[1], mode2.shape[1]

    def body(place_ref, col_ref, depth_ref, signs_ref, mode2_ref, mode3_ref, table_ref, x_ref, o_ref, gram_ref, total):
        k = pl.program_id(0)
        khatri = mode2_ref[...] * mode3_ref[0]
        weighted = khatri * counts(col_ref, depth_ref, k, cols)
        part = lax.dot_general(
            weighted, x_ref[0], (((0,), (1,)), ((), ())), precision=HIGH, preferred_element_type=F32
        )

        gram = lax.dot_general(
            khatri, weighted, (((0,), (0,)), ((), ())), precision=HIGH, preferred_element_type=F32
        )

        @pl.when(k == 0)
        def _():
            total[...] = part
            gram_ref[...] = gram

        @pl.when(k > 0)
        def _():
            total[...] += part
            gram_ref[...] += gram

        @pl.when(k == slices - 1)
        def _():
            rest = total[...] * (signs_ref[...] * factor)
            done = jnp.zeros_like(rest)
            for _ in range(3):
                step = rest.astype(jnp.bfloat16)
                rest = rest - step.astype(F32)
                done = done + jnp.dot(step, table_ref[...], preferred_element_type=F32)
            o_ref[...] = done

    whole = lambda *shape: pl.BlockSpec(shape, lambda k: (0,) * len(shape))
    return chain(
        body, (col, depth, signs, mode2, mode3, table, slab),
        [
            whole(1, samples),
            whole(1, samples),
            whole(1, rows),
            whole(cols, rank),
            pl.BlockSpec((1, 1, rank), lambda k: (k, 0, 0)),
            whole(rows, rows),
            pl.BlockSpec((1, rows, cols), lambda k: (k, 0, 0)),
        ],
        [struct(rank, rows), struct(rank, rank)], [whole(rank, rows), whole(rank, rank)],
        scratch=[pltpu.VMEM((rank, rows), F32)], grid=(slices,), limit=16,
    )


def counts(col_ref, depth_ref, k, cols):
    chosen = jnp.where(depth_ref[...] == k, col_ref[...], -1)
    hits = lax.broadcasted_iota(jnp.int32, (cols, chosen.shape[1]), 0) == chosen
    return jnp.sum(hits.astype(F32), axis=1, keepdims=True)


def fold(chain, which, own, other, more=None):
    rows, cols = own.shape
    square = () if more is None else (more,)
    under = 0 if more is None else more.shape[0]

    def body(place_ref, a_ref, b_ref, *refs):
        o_ref = refs[-1]
        o_ref[:rows] = b_ref[...] + a_ref[...] * sign_of(place_ref[which])
        if under:
            o_ref[rows:] = jnp.zeros((under, cols), F32)
            o_ref[rows:, :under] = refs[0][...]

    return chain(body, (own, other) + square, [VMEM] * (2 + len(square)), [struct(rows + under, cols)], [VMEM])[0]


def add(chain, own, other, rows):
    def body(place_ref, a_ref, b_ref, o_ref):
        o_ref[...] = a_ref[:rows] + b_ref[:rows]

    return chain(body, (own, other), [VMEM] * 2, [struct(rows, own.shape[1])], [VMEM])[0]


def inverse_of(chain, summed, rank, total):
    def body(place_ref, x_ref, o_ref, moment_ref, work):
        moment_ref[...] = x_ref[:rank]
        row = lax.broadcasted_iota(jnp.int32, (rank, 2 * rank), 0)
        col = lax.broadcasted_iota(jnp.int32, (rank, 2 * rank), 1)
        square_row, square_col = row[:, :rank], col[:, :rank]
        eye = jnp.where(square_row == square_col, 1.0, 0.0)
        gram = x_ref[rank:, :rank] * (1.0 / total) + ridge * eye
        work[:, :rank] = gram
        work[:, rank:] = eye

        def step(j, carry):
            now = work[...]
            pivot_row = work[pl.ds(j, 1), :]
            pivot = jnp.sum(jnp.where(col[:1] == j, pivot_row, 0.0), axis=1, keepdims=True)
            pivot_row = pivot_row / pivot
            column = jnp.sum(jnp.where(col == j, now, 0.0), axis=1, keepdims=True)
            work[...] = jnp.where(row == j, pivot_row, now - column * pivot_row)
            return carry

        lax.fori_loop(0, rank, step, 0)
        found = work[:, rank:]
        dot = lambda a, b: jnp.dot(a, b, precision=HIGH, preferred_element_type=F32)
        o_ref[...] = found + dot(found, eye - dot(gram, found))

    return chain(
        body, (summed,), [VMEM], [struct(rank, rank), struct(rank, summed.shape[1])], [VMEM] * 2,
        scratch=[pltpu.VMEM((rank, 2 * rank), F32)],
    )


def swap(value, mask, axis="partner"):
    return lax.ppermute(value, axis, [(s, s ^ mask) for s in range(lax.axis_size(axis))])


def shards(tensor_slab, sign_flips, mode2_factor, mode3_factor, fibre_col, fibre_depth):
    slices, rows, cols = shape = tensor_slab.shape
    parties = lax.axis_size("partner")
    me = lax.axis_index("partner")
    rank = mode2_factor.shape[1]
    total = fibre_col.shape[0] * lax.axis_size("blk")
    scale = 1.0 / math.sqrt(rows * parties)
    signs = sign_flips.astype(F32) * scale
    chain = Chain(jnp.stack([me >> 2, me & 1, (me >> 1) & 1, (me >> 2) & 1, me >> 3]).astype(jnp.int32))
    table = jnp.asarray(hadamard(rows), jnp.bfloat16)

    last = {}

    def go(value, mask, lane, after=()):
        after = tuple(after) + ((last[lane],) if lane in last else ())
        if after:
            value, = gate(chain, (value,), after)
        last[lane] = swap(value, mask)
        return value, last[lane]

    def along_y(pieces, got, *which, after=()):
        got[0] = pieces[0]
        for m in which or (1, 2, 3):
            got[m] = go(pieces[m], 4 * m, m, after)[1]

    def ordered(got):
        return [got[m] for m in range(4)]

    col, depth, mode3 = fibre_col[None], fibre_depth[None], mode3_factor[:, None]

    def small(value, mask, after, axis="partner"):
        value, = gate(chain, (value,), (after,))
        return value, swap(value, mask, axis)

    ct, dt, at, bt, cb, db, ab, bb = ({} for _ in range(8))
    a, c = first(chain, tensor_slab, signs[:, None], table, (0, 2))
    a_other, c_other = swap(a, 1), swap(c, 1)
    d, b = first(chain, tensor_slab, signs[:, None], table, (3, 1))
    d_other, b_other = swap(d, 1), swap(b, 1)
    c = combine_split(chain, 1, c, c_other)
    along_y(c, ct)
    a0 = combine_one(chain, 1, a, a_other, 0)
    a0, a0_other = go(a0, 2, "x0")
    d = combine_split(chain, 1, d, d_other)
    b0, b1 = (combine_one(chain, 1, b, b_other, k) for k in range(2))
    moment, gram = sample(
        chain, col, depth, signs[None], mode2_factor, mode3, tensor_slab, table, 1.0 / math.sqrt(total)
    )
    moment_other = swap(moment, 1)
    along_y(d, dt, 1)
    moment = fold(chain, 1, moment, moment_other, gram)
    a1 = combine_one(chain, 1, a, a_other, 1)
    a1, a1_other = go(a1, 2, "x1")
    along_y(d, dt, 2, 3)
    c = middle(chain, ordered(ct))

    moment, moment_other = small(moment, 1, a0_other, "blk")
    along_y(c, cb, 1, 2)
    moment = add(chain, moment, moment_other, 2 * rank)
    b0, b0_other = go(b0, 2, "x0")
    along_y(c, cb, 3)
    d = middle(chain, ordered(dt))

    moment, moment_other = small(moment, 2, a1_other, "blk")
    a = combine_split_slices(chain, 2, (a0, a1), (a0_other, a1_other))
    along_y(d, db, 1, 2)
    moment = add(chain, moment, moment_other, 2 * rank)
    b1, b1_other = go(b1, 2, "x1")
    along_y(d, db, 3)
    c0, c1 = pack(chain, ordered(cb))

    moment, moment_other = small(moment, 4, b0_other, "blk")
    along_y(a, at, 1, 2)
    summed = add(chain, moment, moment_other, 2 * rank)
    c0, c0_other = go(c0, 2, "x0")
    along_y(a, at, 3)
    d0, d1 = pack(chain, ordered(db))
    inverse, moment = inverse_of(chain, summed, rank, total)

    moment, moment_other = small(moment, 2, b1_other)
    b = combine_split_slices(chain, 2, (b0, b1), (b0_other, b1_other))
    along_y(b, bt, 1, 2)
    moment = fold(chain, 2, moment, moment_other)
    c1, c1_other = go(c1, 2, "x1")
    along_y(b, bt, 3)
    a = middle(chain, ordered(at))

    moment, moment_other = small(moment, 4, c0_other)
    along_y(a, ab, 1, 2)
    moment = fold(chain, 3, moment, moment_other)
    d0, d0_other = go(d0, 2, "x0")
    along_y(a, ab, 3)
    b = middle(chain, ordered(bt))

    moment, moment_other = small(moment, 8, c1_other)
    along_y(b, bb, 1, 2)
    moment = fold(chain, 4, moment, moment_other)
    d1, d1_other = go(d1, 2, "x1")
    along_y(b, bb, 3)
    out = end_slices(chain, 2, (c0, c1), (c0_other, c1_other), 2, shape)
    factor = times_inverse(chain, moment, inverse)
    out = end_mixed(chain, ab, 0, 2, None, None, 0, 0, out, 0)
    out = end_mixed(chain, {m: bb[m] for m in (0, 1)}, 1, 2, d0, d0_other, 3, 0, out, COST)
    out = end_mixed(chain, {2: bb[2]}, 1, 2, None, None, 0, 0, out, COST)
    out = end_mixed(chain, {3: bb[3]}, 1, 2, d1, d1_other, 3, 2, out, COST)
    return (out, factor)


def solution(mesh):
    return jax.shard_map(
        shards,
        mesh=mesh,
        in_specs=(P(None, "partner", "blk"), P("partner"), P("blk", None), P(), P("blk"), P("blk")),
        out_specs=(P(None, "partner", "blk"), P("partner", None)),
        check_vma=False,
    )
```

time: 751 us -> 258 us (0.34)
  waiting for transfers between devices: 574 us -> 103 us
  Pallas kernels: 0 us -> 93 us
  other arithmetic: 56.2 us -> 0.69 us
  starting transfers between devices: 6.55 us -> 53.7 us
  blocking collectives: 43.2 us -> 0 us
  matrix products: 38.5 us -> 0 us
  between operations: 14.2 us -> 1.55 us
  local copies, waits for them, and re-layouts: 18.1 us -> 5.61 us
    ppermute x4 -> x43, waiting for transfers between devices: 502 us -> 103 us  [swap(): lax.ppermute(value, axis, [(s, s ^ mask) for s in range(lax.axis_size(axi...]
    pallas_call x0 -> x64, Pallas kernels: none -> 93 us  [__call__(): pl.pallas_call(inner, out_shape=list(out_shapes) + [struct(8, 128)], grid...]
    psum x1 -> x0, waiting for transfers between devices: 72.6 us -> none  [shards(): moment, gram = lax.psum((moment_part, gram_part), 'blk')]
    ppermute x4 -> x43, starting transfers between devices: 6.52 us -> 53.7 us  [swap(): lax.ppermute(value, axis, [(s, s ^ mask) for s in range(lax.axis_size(axi...]
    psum x1 -> x0, blocking collectives: 43.2 us -> none  [shards(): moment, gram = lax.psum((moment_part, gram_part), 'blk')]
    dot_general x3 -> x0, matrix products: 36.2 us -> none  [the longest x1 33.1 us: shards(): jnp.einsum('ab,kbj->kaj', hadamard_table(local_rows), flipped, precision=...]
    select_n x4 -> x0, other arithmetic: 33.9 us -> none  [the longest x3 33.9 us: shards(): mixed = jnp.where(upper_side, other_half - mixed, mixed + other_half)]
    another operation x5 -> x0, other arithmetic: 12.1 us -> none  [the longest x3 6.52 us: solve_normal(): factor_chol = jnp.linalg.cholesky(gram)]
  transfers between devices with their start and end apart: 5 -> 43, of which waited for: 5 -> 18; matrix products, arithmetic and copies ran while one was open for 3% -> 0% of each run, Pallas kernels for 0% -> 33%
where the time goes in v2:
time: 258 us
  waiting for transfers between devices  103 us (40%)
  Pallas kernels  93 us (36%)
  starting transfers between devices  53.7 us (21%)
  local copies, waits for them, and re-layouts  5.61 us (2%)
    ppermute x43, waiting for transfers between devices, swap(): lax.ppermute(value, axis, [(s, s ^ mask) for s in range(lax.axis_size(axi...  103 us
    pallas_call x64, Pallas kernels, __call__(): pl.pallas_call(inner, out_shape=list(out_shapes) + [struct(8, 128)], grid...  93 us
    ppermute x43, starting transfers between devices, swap(): lax.ppermute(value, axis, [(s, s ^ mask) for s in range(lax.axis_size(axi...  53.7 us
    unnamed x32, local copies, waits for them, and re-layouts  5.38 us
  transfers between devices with their start and end apart: 43, of which 18 were waited for; matrix products, arithmetic and copies ran while one was open for 0% of the time, Pallas kernels for 33%

profile of v2, /device:TPU:0, one launch (start us, length us, event | category | flops | bytes accessed | tf_op | source)
XLA Modules:
  0.0 258.0 jit_solution(1041274606084536451)
XLA Ops:
  2.6 5.2 %shard_map.86 = (f32[2,512,512]{2,1,0:T(8,128)S(1)}, f32[2,512,512]{2,1,0:T(8,128)S(1)}, f32[8,128]{1,0:T(8,128)S(1)}) custom-call(s32[5]{0:T(128)S(1)} %stack.23.place_ref, f32[512,1]{1,0:T(8,128)S(1)} %copy.16.refs_0_, bf16[512,512]{1,0:T(8,128)(2,1)S(1)} %copy-done.3, f32[8,512,512]{2,1,0:T(8,128)} %refs_6_.1), custom_call_target="tpu_custom_call" | custom-call | tf_op jit(solution)/shard_map/pallas_call | solution.py:53
  8.4 6.8 %shard_map.87 = (f32[2,512,512]{2,1,0:T(8,128)}, f32[2,512,512]{2,1,0:T(8,128)}, f32[8,128]{1,0:T(8,128)S(1)}) custom-call(s32[5]{0:T(128)S(1)} %stack.23.place_ref, f32[512,1]{1,0:T(8,128)S(1)} %copy.16.refs_0_, bf16[512,512]{1,0:T(8,128)(2,1)S(1)} %copy-done.3, f32[8,512,512]{2,1,0:T(8,128)} %refs_6_.1, f32[8,128]{1,0:T(8,128)S(1)} %get-tuple-element.159.refs_3_), custom_call_target="tpu_custom_call" | custom-call | tf_op jit(solution)/shard_map/pallas_call | solution.py:53
  33.5 3.4 %copy-done = f32[8,512,512]{2,1,0:T(8,128)S(1)} copy-done((f32[8,512,512]{2,1,0:T(8,128)S(1)}, f32[8,512,512]{2,1,0:T(8,128)}, u32[]{:S(2)}) %copy-start) | copy-done | bytes 8388632
  36.8 11.9 %shard_map.93 = (f32[64,512]{1,0:T(8,128)S(1)}, f32[64,64]{1,0:T(8,128)S(1)}, f32[8,128]{1,0:T(8,128)S(1)}) custom-call(s32[5]{0:T(128)S(1)} %stack.23.place_ref, s32[1,512]{1,0:T(1,128)S(1)} %bitcast.13, s32[1,512]{1,0:T(1,128)S(1)} %bitcast.14, f32[1,512]{1,0:T(1,128)S(1)} %bitcast.11, f32[512,64]{1,0:T(8,128)S(1)} %copy.17.refs_3_, ...), custom_call_target="tpu_custom_call" | custom-call | tf_op jit(solution)/shard_map/pallas_call | solution.py:53
  53.8 4.2 %collective-permute-start.10 = (f32[256,512]{1,0:T(8,128)S(1)}, f32[256,512]{1,0:T(8,128)S(1)}, u32[]{:S(2)}, u32[]{:S(2)}) collective-permute-start(f32[256,512]{1,0:T(8,128)S(1)} %get-tuple-element.191), channel_id=1, source_target_pairs={{0,64},{8,72},{16,80},{24,88},{32,96},{40,104},{48,112},{56,120},{... | collective-permute-start | bytes 1572872 | tf_op jit(solution)/shard_map/ppermute | solution.py:389
  58.0 6.4 %collective-permute-done.8.refs_1_.refs_3_ = f32[256,512]{1,0:T(8,128)S(1)} collective-permute-done((f32[256,512]{1,0:T(8,128)S(1)}, f32[256,512]{1,0:T(8,128)S(1)}, u32[]{:S(2)}, u32[]{:S(2)}) %collective-permute-start.8) | collective-permute-done | bytes 524320 | tf_op jit(solution)/shard_map/ppermute | solution.py:389
  71.1 9.7 %collective-permute-done.10.refs_1_.refs_2_ = f32[256,512]{1,0:T(8,128)S(1)} collective-permute-done((f32[256,512]{1,0:T(8,128)S(1)}, f32[256,512]{1,0:T(8,128)S(1)}, u32[]{:S(2)}, u32[]{:S(2)}) %collective-permute-start.10) | collective-permute-done | bytes 524320 | tf_op jit(solution)/shard_map/ppermute | solution.py:389
  88.1 3.9 %collective-permute-done.13.refs_1_.refs_3_ = f32[256,512]{1,0:T(8,128)S(1)} collective-permute-done((f32[256,512]{1,0:T(8,128)S(1)}, f32[256,512]{1,0:T(8,128)S(1)}, u32[]{:S(2)}, u32[]{:S(2)}) %collective-permute-start.13) | collective-permute-done | bytes 524320 | tf_op jit(solution)/shard_map/ppermute | solution.py:389
  98.5 3.8 %collective-permute-done.15.refs_1_.refs_2_ = f32[256,512]{1,0:T(8,128)S(1)} collective-permute-done((f32[256,512]{1,0:T(8,128)S(1)}, f32[256,512]{1,0:T(8,128)S(1)}, u32[]{:S(2)}, u32[]{:S(2)}) %collective-permute-start.15) | collective-permute-done | bytes 524320 | tf_op jit(solution)/shard_map/ppermute | solution.py:389
  108.5 4.9 %collective-permute-done.19.refs_1_.refs_3_ = f32[256,512]{1,0:T(8,128)S(1)} collective-permute-done((f32[256,512]{1,0:T(8,128)S(1)}, f32[256,512]{1,0:T(8,128)S(1)}, u32[]{:S(2)}, u32[]{:S(2)}) %collective-permute-start.19) | collective-permute-done | bytes 524320 | tf_op jit(solution)/shard_map/ppermute | solution.py:389
  116.8 4.0 %collective-permute-start.20 = (f32[128,512]{1,0:T(8,128)S(1)}, f32[128,512]{1,0:T(8,128)S(1)}, u32[]{:S(2)}, u32[]{:S(2)}) collective-permute-start(f32[128,512]{1,0:T(8,128)S(1)} %get-tuple-element.226.refs_0_), channel_id=1, source_target_pairs={{0,4},{1,5},{2,6},{3,7},{4,0},{5,1},{6,2},{7,3},{8,12},{9,13},{10,... | collective-permute-start | bytes 786440 | tf_op jit(solution)/shard_map/ppermute | solution.py:389
  121.5 11.2 %collective-permute-done.21.refs_1_.refs_2_ = f32[256,512]{1,0:T(8,128)S(1)} collective-permute-done((f32[256,512]{1,0:T(8,128)S(1)}, f32[256,512]{1,0:T(8,128)S(1)}, u32[]{:S(2)}, u32[]{:S(2)}) %collective-permute-start.21) | collective-permute-done | bytes 524320 | tf_op jit(solution)/shard_map/ppermute | solution.py:389
  136.0 4.4 %collective-permute-done.23.refs_1_.refs_3_ = f32[256,512]{1,0:T(8,128)S(1)} collective-permute-done((f32[256,512]{1,0:T(8,128)S(1)}, f32[256,512]{1,0:T(8,128)S(1)}, u32[]{:S(2)}, u32[]{:S(2)}) %collective-permute-start.23) | collective-permute-done | bytes 524320 | tf_op jit(solution)/shard_map/ppermute | solution.py:389
  141.8 7.3 %shard_map.122 = (f32[64,64]{1,0:T(8,128)S(1)}, f32[64,512]{1,0:T(8,128)S(1)}, f32[8,128]{1,0:T(8,128)S(1)}) custom-call(s32[5]{0:T(128)S(1)} %stack.23.place_ref, f32[128,512]{1,0:T(8,128)S(1)} %get-tuple-element.234.refs_0_, f32[8,128]{1,0:T(8,128)S(1)} %get-tuple-element.242.refs_1_), custom_call_target="tpu_custom_call" | custom-call | tf_op jit(solution)/shard_map/pallas_call | solution.py:53
  154.7 4.7 %collective-permute-done.29.refs_1_ = f32[64,512]{1,0:T(8,128)S(1)} collective-permute-done((f32[64,512]{1,0:T(8,128)S(1)}, f32[64,512]{1,0:T(8,128)S(1)}, u32[]{:S(2)}, u32[]{:S(2)}) %collective-permute-start.29) | collective-permute-done | bytes 131104 | tf_op jit(solution)/shard_map/ppermute | solution.py:389
  160.7 3.5 %collective-permute-start.25 = (f32[256,512]{1,0:T(8,128)S(1)}, f32[256,512]{1,0:T(8,128)S(1)}, u32[]{:S(2)}, u32[]{:S(2)}) collective-permute-start(f32[256,512]{1,0:T(8,128)S(1)} %get-tuple-element.250), channel_id=1, source_target_pairs={{0,32},{8,40},{16,48},{24,56},{32,0},{40,8},{48,16},{56,24},{64,96... | collective-permute-start | bytes 1572872 | tf_op jit(solution)/shard_map/ppermute | solution.py:389
  169.1 7.9 %collective-permute-done.25.refs_1_ = f32[256,512]{1,0:T(8,128)S(1)} collective-permute-done((f32[256,512]{1,0:T(8,128)S(1)}, f32[256,512]{1,0:T(8,128)S(1)}, u32[]{:S(2)}, u32[]{:S(2)}) %collective-permute-start.25) | collective-permute-done | bytes 524320 | tf_op jit(solution)/shard_map/ppermute | solution.py:389
  179.8 8.5 %collective-permute-done.27.refs_1_.refs_2_ = f32[256,512]{1,0:T(8,128)S(1)} collective-permute-done((f32[256,512]{1,0:T(8,128)S(1)}, f32[256,512]{1,0:T(8,128)S(1)}, u32[]{:S(2)}, u32[]{:S(2)}) %collective-permute-start.27) | collective-permute-done | bytes 524320 | tf_op jit(solution)/shard_map/ppermute | solution.py:389
  189.0 3.6 %collective-permute-start.36 = (f32[256,512]{1,0:T(8,128)S(1)}, f32[256,512]{1,0:T(8,128)S(1)}, u32[]{:S(2)}, u32[]{:S(2)}) collective-permute-start(f32[256,512]{1,0:T(8,128)S(1)} %get-tuple-element.287), channel_id=1, source_target_pairs={{0,64},{8,72},{16,80},{24,88},{32,96},{40,104},{48,112},{56,120},{... | collective-permute-start | bytes 1572872 | tf_op jit(solution)/shard_map/ppermute | solution.py:389
  192.6 14.8 %collective-permute-done.32.refs_1_ = f32[64,512]{1,0:T(8,128)S(1)} collective-permute-done((f32[64,512]{1,0:T(8,128)S(1)}, f32[64,512]{1,0:T(8,128)S(1)}, u32[]{:S(2)}, u32[]{:S(2)}) %collective-permute-start.32) | collective-permute-done | bytes 131104 | tf_op jit(solution)/shard_map/ppermute | solution.py:389
  223.7 5.1 %collective-permute-done.33.refs_1_.refs_3_ = f32[256,512]{1,0:T(8,128)S(1)} collective-permute-done((f32[256,512]{1,0:T(8,128)S(1)}, f32[256,512]{1,0:T(8,128)S(1)}, u32[]{:S(2)}, u32[]{:S(2)}) %collective-permute-start.33) | collective-permute-done | bytes 524320 | tf_op jit(solution)/shard_map/ppermute | solution.py:389
  236.8 4.4 %collective-permute-done.42.refs_3_ = f32[2,256,512]{2,1,0:T(8,128)} collective-permute-done((f32[2,256,512]{2,1,0:T(8,128)}, f32[2,256,512]{2,1,0:T(8,128)}, u32[]{:S(2)}, u32[]{:S(2)}) %collective-permute-start.42) | collective-permute-done | bytes 1048608 | tf_op jit(solution)/shard_map/ppermute | solution.py:389
  241.1 3.1 %shard_map.147 = (f32[8,512,512]{2,1,0:T(8,128)}, f32[8,128]{1,0:T(8,128)S(1)}) custom-call(s32[5]{0:T(128)S(1)} %stack.23.place_ref, f32[256,512]{1,0:T(8,128)S(1)} %copy-done.8, f32[256,512]{1,0:T(8,128)} %collective-permute-done.41.refs_1_, f32[2,256,512]{2,1,0:T(8,128)} %get-tuple-element.300.refs_2_, ...), custom_call_target="tpu_custom_call", output_to_operand_aliasing={{0}: (5, {})} | custom-call | bytes 30000000 | tf_op jit(solution)/shard_map/pallas_call | solution.py:53
  246.5 8.7 %collective-permute-done.39.refs_2_ = f32[2,256,512]{2,1,0:T(8,128)} collective-permute-done((f32[2,256,512]{2,1,0:T(8,128)S(1)}, f32[2,256,512]{2,1,0:T(8,128)}, u32[]{:S(2)}, u32[]{:S(2)}) %collective-permute-start.39) | collective-permute-done | bytes 1048608 | tf_op jit(solution)/shard_map/ppermute | solution.py:389
  (161 shorter events, 105.2 us)
Async XLA Ops:
  19.7 47.0 %collective-permute-start.4 = (f32[512,512]{1,0:T(8,128)}, f32[512,512]{1,0:T(8,128)S(1)}, u32[]{:S(2)}, u32[]{:S(2)}) collective-permute-start(f32[512,512]{1,0:T(8,128)} %get-tuple-element.169.refs_0_), channel_id=1, source_target_pairs={{0,16},{8,24},{16,0},{24,8},{32,48},{40,56},{48,32},{56,40},{64,80... | collective-permute-start | bytes 3145736 | tf_op jit(solution)/shard_map/ppermute | solution.py:389
  21.4 27.8 %collective-permute-start.6 = (f32[256,512]{1,0:T(8,128)}, f32[256,512]{1,0:T(8,128)}, u32[]{:S(2)}, u32[]{:S(2)}) collective-permute-start(f32[256,512]{1,0:T(8,128)} %get-tuple-element.175), channel_id=1, source_target_pairs={{0,32},{8,40},{16,48},{24,56},{32,0},{40,8},{48,16},{56,24},{64,96... | collective-permute-start | bytes 1572872 | tf_op jit(solution)/shard_map/ppermute | solution.py:389
  22.9 29.7 %collective-permute-start.7 = (f32[256,512]{1,0:T(8,128)}, f32[256,512]{1,0:T(8,128)}, u32[]{:S(2)}, u32[]{:S(2)}) collective-permute-start(f32[256,512]{1,0:T(8,128)} %get-tuple-element.180), channel_id=1, source_target_pairs={{0,64},{8,72},{16,80},{24,88},{32,96},{40,104},{48,112},{56,120},{... | collective-permute-start | bytes 1572872 | tf_op jit(solution)/shard_map/ppermute | solution.py:389
  51.7 41.9 %collective-permute-start.12 = (f32[512,512]{1,0:T(8,128)S(1)}, f32[512,512]{1,0:T(8,128)S(1)}, u32[]{:S(2)}, u32[]{:S(2)}) collective-permute-start(f32[512,512]{1,0:T(8,128)S(1)} %get-tuple-element.200.refs_1_), channel_id=1, source_target_pairs={{0,16},{8,24},{16,0},{24,8},{32,48},{40,56},{48,32},{56,40},{64,80... | collective-permute-start | bytes 3145736 | tf_op jit(solution)/shard_map/ppermute | solution.py:389
  52.2 18.2 %collective-permute-start.11 = (f32[256,512]{1,0:T(8,128)S(1)}, f32[256,512]{1,0:T(8,128)S(1)}, u32[]{:S(2)}, u32[]{:S(2)}) collective-permute-start(f32[256,512]{1,0:T(8,128)S(1)} %get-tuple-element.193), channel_id=1, source_target_pairs={{0,32},{8,40},{16,48},{24,56},{32,0},{40,8},{48,16},{56,24},{64,96... | collective-permute-start | bytes 1572872 | tf_op jit(solution)/shard_map/ppermute | solution.py:389
  53.8 27.0 %collective-permute-start.10 = (f32[256,512]{1,0:T(8,128)S(1)}, f32[256,512]{1,0:T(8,128)S(1)}, u32[]{:S(2)}, u32[]{:S(2)}) collective-permute-start(f32[256,512]{1,0:T(8,128)S(1)} %get-tuple-element.191), channel_id=1, source_target_pairs={{0,64},{8,72},{16,80},{24,88},{32,96},{40,104},{48,112},{56,120},{... | collective-permute-start | bytes 1572872 | tf_op jit(solution)/shard_map/ppermute | solution.py:389
  70.1 21.9 %collective-permute-start.13 = (f32[256,512]{1,0:T(8,128)S(1)}, f32[256,512]{1,0:T(8,128)S(1)}, u32[]{:S(2)}, u32[]{:S(2)}) collective-permute-start(f32[256,512]{1,0:T(8,128)S(1)} %get-tuple-element.203), channel_id=1, source_target_pairs={{0,96},{8,104},{16,112},{24,120},{32,64},{40,72},{48,80},{56,88},{... | collective-permute-start | bytes 1572872 | tf_op jit(solution)/shard_map/ppermute | solution.py:389
  71.0 26.9 %collective-permute-start.16 = (f32[256,512]{1,0:T(8,128)S(1)}, f32[256,512]{1,0:T(8,128)S(1)}, u32[]{:S(2)}, u32[]{:S(2)}) collective-permute-start(f32[256,512]{1,0:T(8,128)S(1)} %get-tuple-element.212), channel_id=1, source_target_pairs={{0,32},{8,40},{16,48},{24,56},{32,0},{40,8},{48,16},{56,24},{64,96... | collective-permute-start | bytes 1572872 | tf_op jit(solution)/shard_map/ppermute | solution.py:389
  85.5 30.7 %collective-permute-start.17 = (f32[512,512]{1,0:T(8,128)S(1)}, f32[512,512]{1,0:T(8,128)S(1)}, u32[]{:S(2)}, u32[]{:S(2)}) collective-permute-start(f32[512,512]{1,0:T(8,128)S(1)} %get-tuple-element.198.refs_0_), channel_id=1, source_target_pairs={{0,16},{8,24},{16,0},{24,8},{32,48},{40,56},{48,32},{56,40},{64,80... | collective-permute-start | bytes 3145736 | tf_op jit(solution)/shard_map/ppermute | solution.py:389
  104.3 44.9 %collective-permute-start.18 = (f32[512,512]{1,0:T(8,128)S(1)}, f32[512,512]{1,0:T(8,128)S(1)}, u32[]{:S(2)}, u32[]{:S(2)}) collective-permute-start(f32[512,512]{1,0:T(8,128)S(1)} %get-tuple-element.218.refs_1_), channel_id=1, source_target_pairs={{0,16},{8,24},{16,0},{24,8},{32,48},{40,56},{48,32},{56,40},{64,80... | collective-permute-start | bytes 3145736 | tf_op jit(solution)/shard_map/ppermute | solution.py:389
  105.8 26.8 %collective-permute-start.21 = (f32[256,512]{1,0:T(8,128)S(1)}, f32[256,512]{1,0:T(8,128)S(1)}, u32[]{:S(2)}, u32[]{:S(2)}) collective-permute-start(f32[256,512]{1,0:T(8,128)S(1)} %get-tuple-element.228), channel_id=1, source_target_pairs={{0,64},{8,72},{16,80},{24,88},{32,96},{40,104},{48,112},{56,120},{... | collective-permute-start | bytes 1572872 | tf_op jit(solution)/shard_map/ppermute | solution.py:389
  114.1 26.3 %collective-permute-start.23 = (f32[256,512]{1,0:T(8,128)S(1)}, f32[256,512]{1,0:T(8,128)S(1)}, u32[]{:S(2)}, u32[]{:S(2)}) collective-permute-start(f32[256,512]{1,0:T(8,128)S(1)} %get-tuple-element.236), channel_id=1, source_target_pairs={{0,96},{8,104},{16,112},{24,120},{32,64},{40,72},{48,80},{56,88},{... | collective-permute-start | bytes 1572872 | tf_op jit(solution)/shard_map/ppermute | solution.py:389
  116.8 17.4 %collective-permute-start.20 = (f32[128,512]{1,0:T(8,128)S(1)}, f32[128,512]{1,0:T(8,128)S(1)}, u32[]{:S(2)}, u32[]{:S(2)}) collective-permute-start(f32[128,512]{1,0:T(8,128)S(1)} %get-tuple-element.226.refs_0_), channel_id=1, source_target_pairs={{0,4},{1,5},{2,6},{3,7},{4,0},{5,1},{6,2},{7,3},{8,12},{9,13},{10,... | collective-permute-start | bytes 786440 | tf_op jit(solution)/shard_map/ppermute | solution.py:389
  121.4 32.0 %collective-permute-start.24 = (f32[256,512]{1,0:T(8,128)S(1)}, f32[256,512]{1,0:T(8,128)S(1)}, u32[]{:S(2)}, u32[]{:S(2)}) collective-permute-start(f32[256,512]{1,0:T(8,128)S(1)} %get-tuple-element.248), channel_id=1, source_target_pairs={{0,32},{8,40},{16,48},{24,56},{32,0},{40,8},{48,16},{56,24},{64,96... | collective-permute-start | bytes 1572872 | tf_op jit(solution)/shard_map/ppermute | solution.py:389
  133.3 20.8 %collective-permute-start.26 = (f32[256,512]{1,0:T(8,128)S(1)}, f32[256,512]{1,0:T(8,128)S(1)}, u32[]{:S(2)}, u32[]{:S(2)}) collective-permute-start(f32[256,512]{1,0:T(8,128)S(1)} %get-tuple-element.252), channel_id=1, source_target_pairs={{0,64},{8,72},{16,80},{24,88},{32,96},{40,104},{48,112},{56,120},{... | collective-permute-start | bytes 1572872 | tf_op jit(solution)/shard_map/ppermute | solution.py:389
  135.4 33.1 %collective-permute-start.31 = (f32[2,256,512]{2,1,0:T(8,128)S(1)}, f32[2,256,512]{2,1,0:T(8,128)S(1)}, u32[]{:S(2)}, u32[]{:S(2)}) collective-permute-start(f32[2,256,512]{2,1,0:T(8,128)S(1)} %get-tuple-element.267.refs_0_), channel_id=1, source_target_pairs={{0,16},{8,24},{16,0},{24,8},{32,48},{40,56},{48,32},{56,40},{64,80... | collective-permute-start | bytes 3145736 | tf_op jit(solution)/shard_map/ppermute | solution.py:389
  160.5 50.6 %collective-permute-start.34 = (f32[2,256,512]{2,1,0:T(8,128)S(1)}, f32[2,256,512]{2,1,0:T(8,128)S(1)}, u32[]{:S(2)}, u32[]{:S(2)}) collective-permute-start(f32[2,256,512]{2,1,0:T(8,128)S(1)} %get-tuple-element.282.refs_1_), channel_id=1, source_target_pairs={{0,16},{8,24},{16,0},{24,8},{32,48},{40,56},{48,32},{56,40},{64,80... | collective-permute-start | bytes 3145736 | tf_op jit(solution)/shard_map/ppermute | solution.py:389
  164.2 24.1 %collective-permute-start.27 = (f32[256,512]{1,0:T(8,128)S(1)}, f32[256,512]{1,0:T(8,128)S(1)}, u32[]{:S(2)}, u32[]{:S(2)}) collective-permute-start(f32[256,512]{1,0:T(8,128)S(1)} %get-tuple-element.254), channel_id=1, source_target_pairs={{0,64},{8,72},{16,80},{24,88},{32,96},{40,104},{48,112},{56,120},{... | collective-permute-start | bytes 1572872 | tf_op jit(solution)/shard_map/ppermute | solution.py:389
  165.8 43.7 %collective-permute-start.30 = (f32[256,512]{1,0:T(8,128)S(1)}, f32[256,512]{1,0:T(8,128)S(1)}, u32[]{:S(2)}, u32[]{:S(2)}) collective-permute-start(f32[256,512]{1,0:T(8,128)S(1)} %get-tuple-element.262), channel_id=1, source_target_pairs={{0,96},{8,104},{16,112},{24,120},{32,64},{40,72},{48,80},{56,88},{... | collective-permute-start | bytes 1572872 | tf_op jit(solution)/shard_map/ppermute | solution.py:389
  177.7 37.6 %collective-permute-start.37 = (f32[256,512]{1,0:T(8,128)S(1)}, f32[256,512]{1,0:T(8,128)S(1)}, u32[]{:S(2)}, u32[]{:S(2)}) collective-permute-start(f32[256,512]{1,0:T(8,128)S(1)} %get-tuple-element.289), channel_id=1, source_target_pairs={{0,32},{8,40},{16,48},{24,56},{32,0},{40,8},{48,16},{56,24},{64,96... | collective-permute-start | bytes 1572872 | tf_op jit(solution)/shard_map/ppermute | solution.py:389
  189.0 27.8 %collective-permute-start.36 = (f32[256,512]{1,0:T(8,128)S(1)}, f32[256,512]{1,0:T(8,128)S(1)}, u32[]{:S(2)}, u32[]{:S(2)}) collective-permute-start(f32[256,512]{1,0:T(8,128)S(1)} %get-tuple-element.287), channel_id=1, source_target_pairs={{0,64},{8,72},{16,80},{24,88},{32,96},{40,104},{48,112},{56,120},{... | collective-permute-start | bytes 1572872 | tf_op jit(solution)/shard_map/ppermute | solution.py:389
  214.7 26.4 %collective-permute-start.42 = (f32[2,256,512]{2,1,0:T(8,128)}, f32[2,256,512]{2,1,0:T(8,128)}, u32[]{:S(2)}, u32[]{:S(2)}) collective-permute-start(f32[2,256,512]{2,1,0:T(8,128)} %get-tuple-element.300.refs_2_), channel_id=1, source_target_pairs={{0,16},{8,24},{16,0},{24,8},{32,48},{40,56},{48,32},{56,40},{64,80... | collective-permute-start | bytes 3145736 | tf_op jit(solution)/shard_map/ppermute | solution.py:389
  220.3 34.9 %collective-permute-start.39 = (f32[2,256,512]{2,1,0:T(8,128)S(1)}, f32[2,256,512]{2,1,0:T(8,128)}, u32[]{:S(2)}, u32[]{:S(2)}) collective-permute-start(f32[2,256,512]{2,1,0:T(8,128)S(1)} %get-tuple-element.296.refs_1_), channel_id=1, source_target_pairs={{0,16},{8,24},{16,0},{24,8},{32,48},{40,56},{48,32},{56,40},{64,80... | collective-permute-start | bytes 3145736 | tf_op jit(solution)/shard_map/ppermute | solution.py:389
  221.5 22.7 %collective-permute-start.40 = (f32[256,512]{1,0:T(8,128)}, f32[256,512]{1,0:T(8,128)}, u32[]{:S(2)}, u32[]{:S(2)}) collective-permute-start(f32[256,512]{1,0:T(8,128)} %get-tuple-element.297), channel_id=1, source_target_pairs={{0,64},{8,72},{16,80},{24,88},{32,96},{40,104},{48,112},{56,120},{... | collective-permute-start | bytes 1572872 | tf_op jit(solution)/shard_map/ppermute | solution.py:389
  (34 other events, 327.0 us)

commit v3 on v2

--- a/solution.py
+++ b/solution.py
@@ -13,7 +13,7 @@
 HIGH = lax.Precision.HIGHEST
 F32 = jnp.float32
 HBM = pl.BlockSpec(memory_space=pltpu.HBM)
-COST = 30_000_000
+COST = 400_000_000
 VMEM = pl.BlockSpec(memory_space=pltpu.VMEM)
 SMEM = pl.BlockSpec(memory_space=pltpu.SMEM)
 
@@ -98,6 +98,21 @@
     )
 
 
+def combine_under(chain, which, own, other, k, more, rank):
+    rows, cols = own.shape[1:]
+
+    def body(place_ref, a_ref, b_ref, more_ref, o_ref):
+        sign = sign_of(place_ref[which])
+
+        def work(at):
+            o_ref[at, :] = b_ref[k, at, :] + a_ref[k, at, :] * sign
+
+        by_rows(rows, 64, work)
+        o_ref[rows:] = more_ref[:rank]
+
+    return chain(body, (own, other, more), [VMEM] * 3, [struct(rows + rank, cols)], [VMEM])[0]
+
+
 def combine_split(chain, which, own, other):
     rows, cols = own.shape[1:]
     half = rows // 2
@@ -237,7 +252,7 @@
     )[0]
 
 
-def end_mixed(chain, parts, group, which, own, other, other_group, first_piece, buffer, cost):
+def end_mixed(chain, parts, group, which, own, other, other_group, first_piece, buffer, cost=0):
     half, cols = buffer.shape[1] // 2, buffer.shape[2]
     names = list(parts)
     n, pieces = len(names), 0 if own is None else own.shape[0]
@@ -245,7 +260,10 @@
 
     def body(place_ref, *refs):
         out, held, sems = refs[n + len(pair) + 1:]
-        copies = [to_place(place_ref, refs[i], out, group, m, half, sems.at[i]) for i, m in enumerate(names)]
+        copies = [
+            to_place(place_ref, refs[i].at[pl.ds(0, half)], out, group, m, half, sems.at[i])
+            for i, m in enumerate(names)
+        ]
         for m in range(pieces):
             def work(at, m=m):
                 held[m, at, :] = refs[n + 1][m, at, :] + refs[n][m, at, :] * sign_of(place_ref[which])
@@ -262,68 +280,77 @@
     )[0]
 
 
-def times_inverse(chain, moment, inverse):
-    rank, rows = moment.shape
-
-    def body(place_ref, a_ref, inverse_ref, o_ref):
+def times_inverse(chain, parts, half, inverse):
+    extra, cols = parts[0].shape[0] - half, parts[0].shape[1]
+
+    def body(place_ref, *refs):
+        inverse_ref, o_ref, moment = refs[4:]
+        for m in range(4):
+            start = pl.multiple_of((place_ref[0] ^ m) * extra, extra)
+            moment[pl.ds(start, extra), :] = refs[m][half:]
         o_ref[...] = lax.dot_general(
-            a_ref[...], inverse_ref[...], (((0,), (0,)), ((), ())), precision=HIGH, preferred_element_type=F32
+            moment[...], inverse_ref[...], (((0,), (0,)), ((), ())), precision=HIGH, preferred_element_type=F32
         )
 
-    return chain(body, (moment, inverse), [VMEM] * 2, [struct(rows, rank)], [VMEM])[0]
+    return chain(
+        body, tuple(parts) + (inverse,), [VMEM] * 5, [struct(cols, inverse.shape[0])], [VMEM],
+        scratch=[pltpu.VMEM((4 * extra, cols), F32)],
+    )[0]
+
+
+def in_three(value):
+    high = value.astype(jnp.bfloat16)
+    rest = value - high.astype(F32)
+    middle_part = rest.astype(jnp.bfloat16)
+    return high, middle_part, (rest - middle_part.astype(F32)).astype(jnp.bfloat16)
 
 
 def sample(chain, col, depth, signs, mode2, mode3, slab, table, factor):
     slices, rows, cols = slab.shape
-    samples, rank = col.shape[1], mode2.shape[1]
-
-    def body(place_ref, col_ref, depth_ref, signs_ref, mode2_ref, mode3_ref, table_ref, x_ref, o_ref, gram_ref, total):
-        k = pl.program_id(0)
-        khatri = mode2_ref[...] * mode3_ref[0]
-        weighted = khatri * counts(col_ref, depth_ref, k, cols)
-        part = lax.dot_general(
-            weighted, x_ref[0], (((0,), (1,)), ((), ())), precision=HIGH, preferred_element_type=F32
-        )
-
-        gram = lax.dot_general(
-            khatri, weighted, (((0,), (0,)), ((), ())), precision=HIGH, preferred_element_type=F32
-        )
-
-        @pl.when(k == 0)
-        def _():
-            total[...] = part
-            gram_ref[...] = gram
-
-        @pl.when(k > 0)
-        def _():
-            total[...] += part
-            gram_ref[...] += gram
-
-        @pl.when(k == slices - 1)
-        def _():
-            rest = total[...] * (signs_ref[...] * factor)
-            done = jnp.zeros_like(rest)
-            for _ in range(3):
-                step = rest.astype(jnp.bfloat16)
-                rest = rest - step.astype(F32)
-                done = done + jnp.dot(step, table_ref[...], preferred_element_type=F32)
-            o_ref[...] = done
-
-    whole = lambda *shape: pl.BlockSpec(shape, lambda k: (0,) * len(shape))
-    return chain(
-        body, (col, depth, signs, mode2, mode3, table, slab),
-        [
-            whole(1, samples),
-            whole(1, samples),
-            whole(1, rows),
-            whole(cols, rank),
-            pl.BlockSpec((1, 1, rank), lambda k: (k, 0, 0)),
-            whole(rows, rows),
-            pl.BlockSpec((1, rows, cols), lambda k: (k, 0, 0)),
+    rank = mode2.shape[1]
+    dot = functools.partial(jnp.dot, preferred_element_type=F32)
+
+    def body(place_ref, col_ref, depth_ref, signs_ref, mode2_ref, mode3_ref, table_ref, x_ref, o_ref, total, gram, held, sems):
+        copies = [pltpu.make_async_copy(x_ref.at[k], held.at[k], sems.at[k]) for k in range(slices)]
+        for copy in copies:
+            copy.start()
+        total[...] = jnp.zeros((rows, rank), F32)
+        gram[...] = jnp.zeros((rank, rank), F32)
+
+        for k, copy in enumerate(copies):
+            khatri = mode2_ref[...] * mode3_ref[k]
+            weighted = khatri * counts(col_ref, depth_ref, k, cols)
+            gram[...] += lax.dot_general(
+                khatri, weighted, (((0,), (0,)), ((), ())), precision=HIGH, preferred_element_type=F32
+            )
+            copy.wait()
+            weights = jnp.concatenate(in_three(weighted), axis=1)
+            x_high, x_middle, x_low = in_three(held[k])
+            most = dot(x_high, weights)
+            some = dot(x_middle, weights[:, : 2 * rank])
+            total[...] += (
+                (dot(x_low, weights[:, :rank]) + some[:, rank:] + most[:, 2 * rank :])
+                + (some[:, :rank] + most[:, rank : 2 * rank])
+                + most[:, :rank]
+            )
+
+        part = total[...].T * (signs_ref[...] * factor)
+        done = jnp.zeros((rank, rows), F32)
+        for piece in in_three(part):
+            done = done + dot(piece, table_ref[...])
+        o_ref[:rank] = done
+        square = gram[...]
+        lines = rank * rank // rows
+        o_ref[rank:] = jnp.concatenate([square[q : q + lines] for q in range(0, rank, lines)], axis=1)
+
+    return chain(
+        body, (col, depth, signs, mode2, mode3, table, slab), [VMEM] * 6 + [HBM], [struct(rank + rank * rank // rows, rows)], [VMEM],
+        scratch=[
+            pltpu.VMEM((rows, rank), F32), pltpu.VMEM((rank, rank), F32),
+            pltpu.VMEM((slices, rows, cols), F32), pltpu.SemaphoreType.DMA((slices,)),
         ],
-        [struct(rank, rows), struct(rank, rank)], [whole(rank, rows), whole(rank, rank)],
-        scratch=[pltpu.VMEM((rank, rows), F32)], grid=(slices,), limit=16,
-    )
+        limit=48,
+    )[0]
 
 
 def counts(col_ref, depth_ref, k, cols):
@@ -332,19 +359,12 @@
     return jnp.sum(hits.astype(F32), axis=1, keepdims=True)
 
 
-def fold(chain, which, own, other, more=None):
-    rows, cols = own.shape
-    square = () if more is None else (more,)
-    under = 0 if more is None else more.shape[0]
-
-    def body(place_ref, a_ref, b_ref, *refs):
-        o_ref = refs[-1]
-        o_ref[:rows] = b_ref[...] + a_ref[...] * sign_of(place_ref[which])
-        if under:
-            o_ref[rows:] = jnp.zeros((under, cols), F32)
-            o_ref[rows:, :under] = refs[0][...]
-
-    return chain(body, (own, other) + square, [VMEM] * (2 + len(square)), [struct(rows + under, cols)], [VMEM])[0]
+def fold(chain, which, own, other, rows):
+    def body(place_ref, a_ref, b_ref, o_ref):
+        o_ref[...] = a_ref[...]
+        o_ref[:rows] = b_ref[:rows] + a_ref[:rows] * sign_of(place_ref[which])
+
+    return chain(body, (own, other), [VMEM] * 2, [struct(*own.shape)], [VMEM])[0]
 
 
 def add(chain, own, other, rows):
@@ -355,13 +375,15 @@
 
 
 def inverse_of(chain, summed, rank, total):
-    def body(place_ref, x_ref, o_ref, moment_ref, work):
-        moment_ref[...] = x_ref[:rank]
+    def body(place_ref, x_ref, o_ref, work):
         row = lax.broadcasted_iota(jnp.int32, (rank, 2 * rank), 0)
         col = lax.broadcasted_iota(jnp.int32, (rank, 2 * rank), 1)
         square_row, square_col = row[:, :rank], col[:, :rank]
         eye = jnp.where(square_row == square_col, 1.0, 0.0)
-        gram = x_ref[rank:, :rank] * (1.0 / total) + ridge * eye
+        packed = x_ref[rank:]
+        lines = packed.shape[0]
+        gram = jnp.concatenate([packed[:, i * rank : (i + 1) * rank] for i in range(rank // lines)], axis=0)
+        gram = gram * (1.0 / total) + ridge * eye
         work[:, :rank] = gram
         work[:, rank:] = eye
 
@@ -380,9 +402,8 @@
         o_ref[...] = found + dot(found, eye - dot(gram, found))
 
     return chain(
-        body, (summed,), [VMEM], [struct(rank, rank), struct(rank, summed.shape[1])], [VMEM] * 2,
-        scratch=[pltpu.VMEM((rank, 2 * rank), F32)],
-    )
+        body, (summed,), [VMEM], [struct(rank, rank)], [VMEM], scratch=[pltpu.VMEM((rank, 2 * rank), F32)],
+    )[0]
 
 
 def swap(value, mask, axis="partner"):
@@ -419,81 +440,61 @@
 
     col, depth, mode3 = fibre_col[None], fibre_depth[None], mode3_factor[:, None]
 
-    def small(value, mask, after, axis="partner"):
-        value, = gate(chain, (value,), (after,))
-        return value, swap(value, mask, axis)
-
-    ct, dt, at, bt, cb, db, ab, bb = ({} for _ in range(8))
+    summed = sample(
+        chain, col, depth, signs[None], mode2_factor, mode3, tensor_slab, table, 1.0 / math.sqrt(total)
+    )
+    summed_other = swap(summed, 1)
     a, c = first(chain, tensor_slab, signs[:, None], table, (0, 2))
     a_other, c_other = swap(a, 1), swap(c, 1)
+    summed = fold(chain, 1, summed, summed_other, rank)
+    summed_other = swap(summed, 1, "blk")
     d, b = first(chain, tensor_slab, signs[:, None], table, (3, 1))
     d_other, b_other = swap(d, 1), swap(b, 1)
+    summed = add(chain, summed, summed_other, summed.shape[0])
+    summed_other = swap(summed, 2, "blk")
+
+    ct, dt, at, bt, cb, db, ab, bb = ({} for _ in range(8))
     c = combine_split(chain, 1, c, c_other)
     along_y(c, ct)
     a0 = combine_one(chain, 1, a, a_other, 0)
     a0, a0_other = go(a0, 2, "x0")
+    summed = add(chain, summed, summed_other, summed.shape[0])
+    summed_other = swap(summed, 4, "blk")
+    a1 = combine_one(chain, 1, a, a_other, 1)
     d = combine_split(chain, 1, d, d_other)
-    b0, b1 = (combine_one(chain, 1, b, b_other, k) for k in range(2))
-    moment, gram = sample(
-        chain, col, depth, signs[None], mode2_factor, mode3, tensor_slab, table, 1.0 / math.sqrt(total)
-    )
-    moment_other = swap(moment, 1)
-    along_y(d, dt, 1)
-    moment = fold(chain, 1, moment, moment_other, gram)
-    a1 = combine_one(chain, 1, a, a_other, 1)
-    a1, a1_other = go(a1, 2, "x1")
-    along_y(d, dt, 2, 3)
+    b0 = combine_one(chain, 1, b, b_other, 0)
+    summed = add(chain, summed, summed_other, summed.shape[0])
+    a1, a1_other = go(gate(chain, (a1,), (summed,))[0], 2, "x1")
+    b1 = combine_under(chain, 1, b, b_other, 1, summed, rank)
+    along_y(d, dt)
     c = middle(chain, ordered(ct))
-
-    moment, moment_other = small(moment, 1, a0_other, "blk")
-    along_y(c, cb, 1, 2)
-    moment = add(chain, moment, moment_other, 2 * rank)
     b0, b0_other = go(b0, 2, "x0")
-    along_y(c, cb, 3)
+    b1, b1_other = go(b1, 2, "x1")
+    along_y(c, cb)
     d = middle(chain, ordered(dt))
-
-    moment, moment_other = small(moment, 2, a1_other, "blk")
     a = combine_split_slices(chain, 2, (a0, a1), (a0_other, a1_other))
-    along_y(d, db, 1, 2)
-    moment = add(chain, moment, moment_other, 2 * rank)
-    b1, b1_other = go(b1, 2, "x1")
-    along_y(d, db, 3)
+    along_y(d, db)
     c0, c1 = pack(chain, ordered(cb))
-
-    moment, moment_other = small(moment, 4, b0_other, "blk")
-    along_y(a, at, 1, 2)
-    summed = add(chain, moment, moment_other, 2 * rank)
     c0, c0_other = go(c0, 2, "x0")
-    along_y(a, at, 3)
+    c1, c1_other = go(c1, 2, "x1")
+    along_y(a, at)
     d0, d1 = pack(chain, ordered(db))
-    inverse, moment = inverse_of(chain, summed, rank, total)
-
-    moment, moment_other = small(moment, 2, b1_other)
     b = combine_split_slices(chain, 2, (b0, b1), (b0_other, b1_other))
-    along_y(b, bt, 1, 2)
-    moment = fold(chain, 2, moment, moment_other)
-    c1, c1_other = go(c1, 2, "x1")
-    along_y(b, bt, 3)
+    along_y(b, bt, 1)
+    inverse = inverse_of(chain, summed, rank, total)
+    along_y(b, bt, 2, 3)
     a = middle(chain, ordered(at))
-
-    moment, moment_other = small(moment, 4, c0_other)
-    along_y(a, ab, 1, 2)
-    moment = fold(chain, 3, moment, moment_other)
     d0, d0_other = go(d0, 2, "x0")
-    along_y(a, ab, 3)
+    d1, d1_other = go(d1, 2, "x1")
+    along_y(a, ab)
     b = middle(chain, ordered(bt))
-
-    moment, moment_other = small(moment, 8, c1_other)
-    along_y(b, bb, 1, 2)
-    moment = fold(chain, 4, moment, moment_other)
-    d1, d1_other = go(d1, 2, "x1")
-    along_y(b, bb, 3)
+    along_y(b, bb)
     out = end_slices(chain, 2, (c0, c1), (c0_other, c1_other), 2, shape)
-    factor = times_inverse(chain, moment, inverse)
-    out = end_mixed(chain, ab, 0, 2, None, None, 0, 0, out, 0)
+    out = end_mixed(chain, ab, 0, 2, None, None, 0, 0, out)
     out = end_mixed(chain, {m: bb[m] for m in (0, 1)}, 1, 2, d0, d0_other, 3, 0, out, COST)
     out = end_mixed(chain, {2: bb[2]}, 1, 2, None, None, 0, 0, out, COST)
     out = end_mixed(chain, {3: bb[3]}, 1, 2, d1, d1_other, 3, 2, out, COST)
+    factor = times_inverse(chain, ordered(bb), rows // 2, inverse)
     return (out, factor)
 
 

time: 258 us -> 245 us (0.950)
  Pallas kernels: 93 us -> 68 us
  waiting for transfers between devices: 103 us -> 116 us
    pallas_call x64 -> x56, Pallas kernels: 93 us -> 68 us  [__call__(): pl.pallas_call(inner, out_shape=list(out_shapes) + [struct(8, 128)], grid...]
    ppermute x43 -> x40, waiting for transfers between devices: 103 us -> 116 us  [swap(): lax.ppermute(value, axis, [(s, s ^ mask) for s in range(lax.axis_size(axi...]
    unnamed x32 -> x12, local copies, waits for them, and re-layouts: 5.38 us -> 4.89 us
    ppermute x43 -> x40, starting transfers between devices: 53.7 us -> 53.6 us  [swap(): lax.ppermute(value, axis, [(s, s ^ mask) for s in range(lax.axis_size(axi...]
  transfers between devices with their start and end apart: 43 -> 40, of which waited for: 18 -> 23; matrix products, arithmetic and copies ran while one was open for 0% -> 0% of each run, Pallas kernels for 33% -> 23%
where the time goes in v3:
time: 245 us
  waiting for transfers between devices  116 us (47%)
  Pallas kernels  68 us (28%)
  starting transfers between devices  53.6 us (22%)
  local copies, waits for them, and re-layouts  5.13 us (2%)
    ppermute x40, waiting for transfers between devices, swap(): lax.ppermute(value, axis, [(s, s ^ mask) for s in range(lax.axis_size(axi...  116 us
    pallas_call x56, Pallas kernels, __call__(): pl.pallas_call(inner, out_shape=list(out_shapes) + [struct(8, 128)], grid...  68 us
    ppermute x40, starting transfers between devices, swap(): lax.ppermute(value, axis, [(s, s ^ mask) for s in range(lax.axis_size(axi...  53.6 us
  transfers between devices with their start and end apart: 40, of which 23 were waited for; matrix products, arithmetic and copies ran while one was open for 0% of the time, Pallas kernels for 23%

profile of v3, /device:TPU:0, one launch (start us, length us, event | category | flops | bytes accessed | tf_op | source)
XLA Modules:
  0.0 244.9 jit_solution(41050333796614724)
XLA Ops:
  5.5 9.2 %shard_map.86 = (f32[72,512]{1,0:T(8,128)S(1)}, f32[8,128]{1,0:T(8,128)S(1)}) custom-call(s32[5]{0:T(128)S(1)} %stack.23.place_ref, s32[1,512]{1,0:T(1,128)S(1)} %bitcast.13, s32[1,512]{1,0:T(1,128)S(1)} %bitcast.14, f32[1,512]{1,0:T(1,128)S(1)} %bitcast.10, f32[512,64]{1,0:T(8,128)S(1)} %copy.15.refs_3_, f32[8,1,64]{2,1,0:T(1,128)S(1)} %bitcast.12, ...), custom_call_target="tpu_custom_call" | custom-call | tf_op jit(solution)/shard_map/pallas_call | solution.py:53
  15.0 5.1 %shard_map.87 = (f32[2,512,512]{2,1,0:T(8,128)S(1)}, f32[2,512,512]{2,1,0:T(8,128)S(1)}, f32[8,128]{1,0:T(8,128)S(1)}) custom-call(s32[5]{0:T(128)S(1)} %stack.23.place_ref, f32[512,1]{1,0:T(8,128)S(1)} %copy.17.refs_0_, bf16[512,512]{1,0:T(8,128)(2,1)S(1)} %copy-done.1, f32[8,512,512]{2,1,0:T(8,128)} %refs_2_.3, f32[8,128]{1,0:T(8,128)S(1)} %get-tuple-element.142.refs_3_), custom_call_target="tpu_custom_call" | custom-call | tf_op jit(solution)/shard_map/pallas_call | solution.py:53
  21.5 5.1 %shard_map.89 = (f32[2,512,512]{2,1,0:T(8,128)S(1)}, f32[2,512,512]{2,1,0:T(8,128)S(1)}, f32[8,128]{1,0:T(8,128)S(1)}) custom-call(s32[5]{0:T(128)S(1)} %stack.23.place_ref, f32[512,1]{1,0:T(8,128)S(1)} %copy.17.refs_0_, bf16[512,512]{1,0:T(8,128)(2,1)S(1)} %copy-done.1, f32[8,512,512]{2,1,0:T(8,128)} %refs_2_.3, f32[8,128]{1,0:T(8,128)S(1)} %get-tuple-element.144.refs_3_), custom_call_target="tpu_custom_call" | custom-call | tf_op jit(solution)/shard_map/pallas_call | solution.py:53
  27.3 3.1 %collective-permute-start.4 = (f32[72,512]{1,0:T(8,128)S(1)}, f32[72,512]{1,0:T(8,128)S(1)}, u32[]{:S(2)}, u32[]{:S(2)}) collective-permute-start(f32[72,512]{1,0:T(8,128)S(1)} %get-tuple-element.148.refs_0_), channel_id=1, source_target_pairs={{0,1},{1,0},{2,3},{3,2},{4,5},{5,4},{6,7},{7,6},{8,9},{9,8},{10,11... | collective-permute-start | bytes 442376 | tf_op jit(solution)/shard_map/ppermute | solution.py:410
  30.4 4.4 %collective-permute-done.4.refs_1_ = f32[72,512]{1,0:T(8,128)S(1)} collective-permute-done((f32[72,512]{1,0:T(8,128)S(1)}, f32[72,512]{1,0:T(8,128)S(1)}, u32[]{:S(2)}, u32[]{:S(2)}) %collective-permute-start.4) | collective-permute-done | bytes 147488 | tf_op jit(solution)/shard_map/ppermute | solution.py:410
  41.4 3.8 %collective-permute-start.11 = (f32[72,512]{1,0:T(8,128)S(1)}, f32[72,512]{1,0:T(8,128)S(1)}, u32[]{:S(2)}, u32[]{:S(2)}) collective-permute-start(f32[72,512]{1,0:T(8,128)S(1)} %get-tuple-element.167.refs_0_), channel_id=1, source_target_pairs={{0,4},{1,5},{2,6},{3,7},{4,0},{5,1},{6,2},{7,3},{8,12},{9,13},{10,... | collective-permute-start | bytes 442376 | tf_op jit(solution)/shard_map/ppermute | solution.py:410
  52.8 2.9 %collective-permute-start.9 = (f32[256,512]{1,0:T(8,128)S(1)}, f32[256,512]{1,0:T(8,128)S(1)}, u32[]{:S(2)}, u32[]{:S(2)}) collective-permute-start(f32[256,512]{1,0:T(8,128)S(1)} %get-tuple-element.162), channel_id=1, source_target_pairs={{0,64},{8,72},{16,80},{24,88},{32,96},{40,104},{48,112},{56,120},{... | collective-permute-start | bytes 1572872 | tf_op jit(solution)/shard_map/ppermute | solution.py:410
  56.6 9.5 %collective-permute-done.8.refs_1_ = f32[256,512]{1,0:T(8,128)S(1)} collective-permute-done((f32[256,512]{1,0:T(8,128)S(1)}, f32[256,512]{1,0:T(8,128)S(1)}, u32[]{:S(2)}, u32[]{:S(2)}) %collective-permute-start.8) | collective-permute-done | bytes 524320 | tf_op jit(solution)/shard_map/ppermute | solution.py:410
  68.3 11.4 %collective-permute-done.9.refs_1_.refs_2_ = f32[256,512]{1,0:T(8,128)S(1)} collective-permute-done((f32[256,512]{1,0:T(8,128)S(1)}, f32[256,512]{1,0:T(8,128)S(1)}, u32[]{:S(2)}, u32[]{:S(2)}) %collective-permute-start.9) | collective-permute-done | bytes 524320 | tf_op jit(solution)/shard_map/ppermute | solution.py:410
  81.8 2.3 collective-permute-start.17
  85.7 5.0 %collective-permute-done.12.refs_1_.refs_3_ = f32[512,512]{1,0:T(8,128)S(1)} collective-permute-done((f32[512,512]{1,0:T(8,128)S(1)}, f32[512,512]{1,0:T(8,128)S(1)}, u32[]{:S(2)}, u32[]{:S(2)}) %collective-permute-start.12) | collective-permute-done | bytes 1048608 | tf_op jit(solution)/shard_map/ppermute | solution.py:410
  95.8 5.0 %collective-permute-done.16.refs_1_.refs_2_ = f32[256,512]{1,0:T(8,128)S(1)} collective-permute-done((f32[256,512]{1,0:T(8,128)S(1)}, f32[256,512]{1,0:T(8,128)S(1)}, u32[]{:S(2)}, u32[]{:S(2)}) %collective-permute-start.16) | collective-permute-done | bytes 524320 | tf_op jit(solution)/shard_map/ppermute | solution.py:410
  106.9 2.7 %collective-permute-done.18.refs_1_ = f32[256,512]{1,0:T(8,128)S(1)} collective-permute-done((f32[256,512]{1,0:T(8,128)S(1)}, f32[256,512]{1,0:T(8,128)S(1)}, u32[]{:S(2)}, u32[]{:S(2)}) %collective-permute-start.18) | collective-permute-done | bytes 524320 | tf_op jit(solution)/shard_map/ppermute | solution.py:410
  111.9 11.4 %collective-permute-done.20.refs_1_.refs_2_ = f32[256,512]{1,0:T(8,128)S(1)} collective-permute-done((f32[256,512]{1,0:T(8,128)S(1)}, f32[256,512]{1,0:T(8,128)S(1)}, u32[]{:S(2)}, u32[]{:S(2)}) %collective-permute-start.20) | collective-permute-done | bytes 524320 | tf_op jit(solution)/shard_map/ppermute | solution.py:410
  128.3 10.6 %collective-permute-done.13.refs_1_.refs_2_ = f32[512,512]{1,0:T(8,128)S(1)} collective-permute-done((f32[512,512]{1,0:T(8,128)S(1)}, f32[512,512]{1,0:T(8,128)S(1)}, u32[]{:S(2)}, u32[]{:S(2)}) %collective-permute-start.13) | collective-permute-done | bytes 1048608 | tf_op jit(solution)/shard_map/ppermute | solution.py:410
  153.1 2.6 %collective-permute-done.24.refs_1_ = f32[256,512]{1,0:T(8,128)S(1)} collective-permute-done((f32[256,512]{1,0:T(8,128)S(1)}, f32[256,512]{1,0:T(8,128)S(1)}, u32[]{:S(2)}, u32[]{:S(2)}) %collective-permute-start.24) | collective-permute-done | bytes 524320 | tf_op jit(solution)/shard_map/ppermute | solution.py:410
  156.4 7.3 %shard_map.123 = (f32[64,64]{1,0:T(8,128)S(1)}, f32[8,128]{1,0:T(8,128)S(1)}) custom-call(s32[5]{0:T(128)S(1)} %stack.23.place_ref, f32[72,512]{1,0:T(8,128)S(1)} %get-tuple-element.169.refs_1_.refs_2_.refs_0_, f32[8,128]{1,0:T(8,128)S(1)} %get-tuple-element.229.refs_1_), custom_call_target="tpu_custom_call" | custom-call | tf_op jit(solution)/shard_map/pallas_call | solution.py:53
  165.3 4.2 %collective-permute-done.26.refs_1_.refs_2_ = f32[256,512]{1,0:T(8,128)S(1)} collective-permute-done((f32[256,512]{1,0:T(8,128)S(1)}, f32[256,512]{1,0:T(8,128)S(1)}, u32[]{:S(2)}, u32[]{:S(2)}) %collective-permute-start.26) | collective-permute-done | bytes 524320 | tf_op jit(solution)/shard_map/ppermute | solution.py:410
  171.5 2.3 collective-permute-start.29
  176.2 16.1 %collective-permute-done.30.refs_1_.refs_3_ = f32[2,256,512]{2,1,0:T(8,128)S(1)} collective-permute-done((f32[2,256,512]{2,1,0:T(8,128)S(1)}, f32[2,256,512]{2,1,0:T(8,128)S(1)}, u32[]{:S(2)}, u32[]{:S(2)}) %collective-permute-start.30) | collective-permute-done | bytes 1048608 | tf_op jit(solution)/shard_map/ppermute | solution.py:410
  202.9 5.8 %collective-permute-done.34.refs_1_ = f32[256,512]{1,0:T(8,128)S(1)} collective-permute-done((f32[256,512]{1,0:T(8,128)S(1)}, f32[256,512]{1,0:T(8,128)S(1)}, u32[]{:S(2)}, u32[]{:S(2)}) %collective-permute-start.34) | collective-permute-done | bytes 524320 | tf_op jit(solution)/shard_map/ppermute | solution.py:410
  210.1 10.4 %collective-permute-done.33.refs_1_.refs_2_ = f32[256,512]{1,0:T(8,128)S(1)} collective-permute-done((f32[256,512]{1,0:T(8,128)S(1)}, f32[256,512]{1,0:T(8,128)S(1)}, u32[]{:S(2)}, u32[]{:S(2)}) %collective-permute-start.33) | collective-permute-done | bytes 524320 | tf_op jit(solution)/shard_map/ppermute | solution.py:410
  228.4 2.8 %collective-permute-done.38.refs_1_ = f32[272,512]{1,0:T(8,128)S(1)} collective-permute-done((f32[272,512]{1,0:T(8,128)S(1)}, f32[272,512]{1,0:T(8,128)S(1)}, u32[]{:S(2)}, u32[]{:S(2)}) %collective-permute-start.38) | collective-permute-done | bytes 557088 | tf_op jit(solution)/shard_map/ppermute | solution.py:410
  233.1 4.3 %collective-permute-done.37.refs_0_.refs_2_ = f32[272,512]{1,0:T(8,128)S(1)} collective-permute-done((f32[272,512]{1,0:T(8,128)S(1)}, f32[272,512]{1,0:T(8,128)S(1)}, u32[]{:S(2)}, u32[]{:S(2)}) %collective-permute-start.37) | collective-permute-done | bytes 557088 | tf_op jit(solution)/shard_map/ppermute | solution.py:410
  (127 shorter events, 96.5 us)
Async XLA Ops:
  27.0 21.3 %collective-permute-start.1 = (f32[2,512,512]{2,1,0:T(8,128)S(1)}, f32[2,512,512]{2,1,0:T(8,128)S(1)}, u32[]{:S(2)}, u32[]{:S(2)}) collective-permute-start(f32[2,512,512]{2,1,0:T(8,128)S(1)} %get-tuple-element.145.refs_0_), channel_id=1, source_target_pairs={{0,8},{8,0},{16,24},{24,16},{32,40},{40,32},{48,56},{56,48},{64,72... | collective-permute-start | bytes 6291464 | tf_op jit(solution)/shard_map/ppermute | solution.py:410
  45.2 39.8 %collective-permute-start.7 = (f32[512,512]{1,0:T(8,128)S(1)}, f32[512,512]{1,0:T(8,128)S(1)}, u32[]{:S(2)}, u32[]{:S(2)}) collective-permute-start(f32[512,512]{1,0:T(8,128)S(1)} %get-tuple-element.159.refs_0_), channel_id=1, source_target_pairs={{0,16},{8,24},{16,0},{24,8},{32,48},{40,56},{48,32},{56,40},{64,80... | collective-permute-start | bytes 3145736 | tf_op jit(solution)/shard_map/ppermute | solution.py:410
  50.3 40.4 %collective-permute-start.12 = (f32[512,512]{1,0:T(8,128)S(1)}, f32[512,512]{1,0:T(8,128)S(1)}, u32[]{:S(2)}, u32[]{:S(2)}) collective-permute-start(f32[512,512]{1,0:T(8,128)S(1)} %get-tuple-element.180.refs_1_), channel_id=1, source_target_pairs={{0,16},{8,24},{16,0},{24,8},{32,48},{40,56},{48,32},{56,40},{64,80... | collective-permute-start | bytes 3145736 | tf_op jit(solution)/shard_map/ppermute | solution.py:410
  52.8 27.0 %collective-permute-start.9 = (f32[256,512]{1,0:T(8,128)S(1)}, f32[256,512]{1,0:T(8,128)S(1)}, u32[]{:S(2)}, u32[]{:S(2)}) collective-permute-start(f32[256,512]{1,0:T(8,128)S(1)} %get-tuple-element.162), channel_id=1, source_target_pairs={{0,64},{8,72},{16,80},{24,88},{32,96},{40,104},{48,112},{56,120},{... | collective-permute-start | bytes 1572872 | tf_op jit(solution)/shard_map/ppermute | solution.py:410
  55.7 25.5 %collective-permute-start.10 = (f32[256,512]{1,0:T(8,128)S(1)}, f32[256,512]{1,0:T(8,128)S(1)}, u32[]{:S(2)}, u32[]{:S(2)}) collective-permute-start(f32[256,512]{1,0:T(8,128)S(1)} %get-tuple-element.163), channel_id=1, source_target_pairs={{0,96},{8,104},{16,112},{24,120},{32,64},{40,72},{48,80},{56,88},{... | collective-permute-start | bytes 1572872 | tf_op jit(solution)/shard_map/ppermute | solution.py:410
  66.7 26.9 %collective-permute-start.15 = (f32[256,512]{1,0:T(8,128)S(1)}, f32[256,512]{1,0:T(8,128)S(1)}, u32[]{:S(2)}, u32[]{:S(2)}) collective-permute-start(f32[256,512]{1,0:T(8,128)S(1)} %get-tuple-element.184), channel_id=1, source_target_pairs={{0,32},{8,40},{16,48},{24,56},{32,0},{40,8},{48,16},{56,24},{64,96... | collective-permute-start | bytes 1572872 | tf_op jit(solution)/shard_map/ppermute | solution.py:410
  91.4 48.1 %collective-permute-start.14 = (f32[576,512]{1,0:T(8,128)S(1)}, f32[576,512]{1,0:T(8,128)S(1)}, u32[]{:S(2)}, u32[]{:S(2)}) collective-permute-start(f32[576,512]{1,0:T(8,128)S(1)} %get-tuple-element.182.refs_1_), channel_id=1, source_target_pairs={{0,16},{8,24},{16,0},{24,8},{32,48},{40,56},{48,32},{56,40},{64,80... | collective-permute-start | bytes 3538952 | tf_op jit(solution)/shard_map/ppermute | solution.py:410
  93.0 45.9 %collective-permute-start.13 = (f32[512,512]{1,0:T(8,128)S(1)}, f32[512,512]{1,0:T(8,128)S(1)}, u32[]{:S(2)}, u32[]{:S(2)}) collective-permute-start(f32[512,512]{1,0:T(8,128)S(1)} %get-tuple-element.178.refs_0_), channel_id=1, source_target_pairs={{0,16},{8,24},{16,0},{24,8},{32,48},{40,56},{48,32},{56,40},{64,80... | collective-permute-start | bytes 3145736 | tf_op jit(solution)/shard_map/ppermute | solution.py:410
  101.5 21.9 %collective-permute-start.20 = (f32[256,512]{1,0:T(8,128)S(1)}, f32[256,512]{1,0:T(8,128)S(1)}, u32[]{:S(2)}, u32[]{:S(2)}) collective-permute-start(f32[256,512]{1,0:T(8,128)S(1)} %get-tuple-element.201), channel_id=1, source_target_pairs={{0,64},{8,72},{16,80},{24,88},{32,96},{40,104},{48,112},{56,120},{... | collective-permute-start | bytes 1572872 | tf_op jit(solution)/shard_map/ppermute | solution.py:410
  103.5 21.5 %collective-permute-start.22 = (f32[256,512]{1,0:T(8,128)S(1)}, f32[256,512]{1,0:T(8,128)S(1)}, u32[]{:S(2)}, u32[]{:S(2)}) collective-permute-start(f32[256,512]{1,0:T(8,128)S(1)} %get-tuple-element.205), channel_id=1, source_target_pairs={{0,96},{8,104},{16,112},{24,120},{32,64},{40,72},{48,80},{56,88},{... | collective-permute-start | bytes 1572872 | tf_op jit(solution)/shard_map/ppermute | solution.py:410
  110.3 29.9 %collective-permute-start.19 = (f32[256,512]{1,0:T(8,128)S(1)}, f32[256,512]{1,0:T(8,128)S(1)}, u32[]{:S(2)}, u32[]{:S(2)}) collective-permute-start(f32[256,512]{1,0:T(8,128)S(1)} %get-tuple-element.199), channel_id=1, source_target_pairs={{0,32},{8,40},{16,48},{24,56},{32,0},{40,8},{48,16},{56,24},{64,96... | collective-permute-start | bytes 1572872 | tf_op jit(solution)/shard_map/ppermute | solution.py:410
  125.7 21.8 %collective-permute-start.23 = (f32[256,512]{1,0:T(8,128)S(1)}, f32[256,512]{1,0:T(8,128)S(1)}, u32[]{:S(2)}, u32[]{:S(2)}) collective-permute-start(f32[256,512]{1,0:T(8,128)S(1)} %get-tuple-element.207), channel_id=1, source_target_pairs={{0,96},{8,104},{16,112},{24,120},{32,64},{40,72},{48,80},{56,88},{... | collective-permute-start | bytes 1572872 | tf_op jit(solution)/shard_map/ppermute | solution.py:410
  145.3 24.2 %collective-permute-start.26 = (f32[256,512]{1,0:T(8,128)S(1)}, f32[256,512]{1,0:T(8,128)S(1)}, u32[]{:S(2)}, u32[]{:S(2)}) collective-permute-start(f32[256,512]{1,0:T(8,128)S(1)} %get-tuple-element.228), channel_id=1, source_target_pairs={{0,64},{8,72},{16,80},{24,88},{32,96},{40,104},{48,112},{56,120},{... | collective-permute-start | bytes 1572872 | tf_op jit(solution)/shard_map/ppermute | solution.py:410
  148.1 22.7 %collective-permute-start.28 = (f32[256,512]{1,0:T(8,128)S(1)}, f32[256,512]{1,0:T(8,128)S(1)}, u32[]{:S(2)}, u32[]{:S(2)}) collective-permute-start(f32[256,512]{1,0:T(8,128)S(1)} %get-tuple-element.233), channel_id=1, source_target_pairs={{0,96},{8,104},{16,112},{24,120},{32,64},{40,72},{48,80},{56,88},{... | collective-permute-start | bytes 1572872 | tf_op jit(solution)/shard_map/ppermute | solution.py:410
  149.5 26.1 %collective-permute-start.31 = (f32[2,256,512]{2,1,0:T(8,128)S(1)}, f32[2,256,512]{2,1,0:T(8,128)S(1)}, u32[]{:S(2)}, u32[]{:S(2)}) collective-permute-start(f32[2,256,512]{2,1,0:T(8,128)S(1)} %get-tuple-element.244.refs_0_), channel_id=1, source_target_pairs={{0,16},{8,24},{16,0},{24,8},{32,48},{40,56},{48,32},{56,40},{64,80... | collective-permute-start | bytes 3145736 | tf_op jit(solution)/shard_map/ppermute | solution.py:410
  151.0 41.3 %collective-permute-start.30 = (f32[2,256,512]{2,1,0:T(8,128)S(1)}, f32[2,256,512]{2,1,0:T(8,128)S(1)}, u32[]{:S(2)}, u32[]{:S(2)}) collective-permute-start(f32[2,256,512]{2,1,0:T(8,128)S(1)} %get-tuple-element.242.refs_1_), channel_id=1, source_target_pairs={{0,16},{8,24},{16,0},{24,8},{32,48},{40,56},{48,32},{56,40},{64,80... | collective-permute-start | bytes 3145736 | tf_op jit(solution)/shard_map/ppermute | solution.py:410
  163.7 29.2 %collective-permute-start.25 = (f32[272,512]{1,0:T(8,128)S(1)}, f32[272,512]{1,0:T(8,128)S(1)}, u32[]{:S(2)}, u32[]{:S(2)}) collective-permute-start(f32[272,512]{1,0:T(8,128)S(1)} %get-tuple-element.226), channel_id=1, source_target_pairs={{0,32},{8,40},{16,48},{24,56},{32,0},{40,8},{48,16},{56,24},{64,96... | collective-permute-start | bytes 1671176 | tf_op jit(solution)/shard_map/ppermute | solution.py:410
  170.1 24.4 %collective-permute-start.27 = (f32[272,512]{1,0:T(8,128)S(1)}, f32[272,512]{1,0:T(8,128)S(1)}, u32[]{:S(2)}, u32[]{:S(2)}) collective-permute-start(f32[272,512]{1,0:T(8,128)S(1)} %get-tuple-element.231), channel_id=1, source_target_pairs={{0,64},{8,72},{16,80},{24,88},{32,96},{40,104},{48,112},{56,120},{... | collective-permute-start | bytes 1671176 | tf_op jit(solution)/shard_map/ppermute | solution.py:410
  171.5 25.6 %collective-permute-start.29 = (f32[272,512]{1,0:T(8,128)S(1)}, f32[272,512]{1,0:T(8,128)S(1)}, u32[]{:S(2)}, u32[]{:S(2)}) collective-permute-start(f32[272,512]{1,0:T(8,128)S(1)} %get-tuple-element.235), channel_id=1, source_target_pairs={{0,96},{8,104},{16,112},{24,120},{32,64},{40,72},{48,80},{56,88},{... | collective-permute-start | bytes 1671176 | tf_op jit(solution)/shard_map/ppermute | solution.py:410
  195.1 25.4 %collective-permute-start.33 = (f32[256,512]{1,0:T(8,128)S(1)}, f32[256,512]{1,0:T(8,128)S(1)}, u32[]{:S(2)}, u32[]{:S(2)}) collective-permute-start(f32[256,512]{1,0:T(8,128)S(1)} %get-tuple-element.254), channel_id=1, source_target_pairs={{0,64},{8,72},{16,80},{24,88},{32,96},{40,104},{48,112},{56,120},{... | collective-permute-start | bytes 1572872 | tf_op jit(solution)/shard_map/ppermute | solution.py:410
  197.7 25.2 %collective-permute-start.32 = (f32[256,512]{1,0:T(8,128)S(1)}, f32[256,512]{1,0:T(8,128)S(1)}, u32[]{:S(2)}, u32[]{:S(2)}) collective-permute-start(f32[256,512]{1,0:T(8,128)S(1)} %get-tuple-element.252), channel_id=1, source_target_pairs={{0,96},{8,104},{16,112},{24,120},{32,64},{40,72},{48,80},{56,88},{... | collective-permute-start | bytes 1572872 | tf_op jit(solution)/shard_map/ppermute | solution.py:410
  200.0 28.4 %collective-permute-start.39 = (f32[2,256,512]{2,1,0:T(8,128)S(1)}, f32[2,256,512]{2,1,0:T(8,128)S(1)}, u32[]{:S(2)}, u32[]{:S(2)}) collective-permute-start(f32[2,256,512]{2,1,0:T(8,128)S(1)} %get-tuple-element.265.refs_2_), channel_id=1, source_target_pairs={{0,16},{8,24},{16,0},{24,8},{32,48},{40,56},{48,32},{56,40},{64,80... | collective-permute-start | bytes 3145736 | tf_op jit(solution)/shard_map/ppermute | solution.py:410
  201.5 39.5 %collective-permute-start.36 = (f32[2,256,512]{2,1,0:T(8,128)S(1)}, f32[2,256,512]{2,1,0:T(8,128)S(1)}, u32[]{:S(2)}, u32[]{:S(2)}) collective-permute-start(f32[2,256,512]{2,1,0:T(8,128)S(1)} %get-tuple-element.261.refs_1_), channel_id=1, source_target_pairs={{0,16},{8,24},{16,0},{24,8},{32,48},{40,56},{48,32},{56,40},{64,80... | collective-permute-start | bytes 3145736 | tf_op jit(solution)/shard_map/ppermute | solution.py:410
  209.3 21.9 %collective-permute-start.38 = (f32[272,512]{1,0:T(8,128)S(1)}, f32[272,512]{1,0:T(8,128)S(1)}, u32[]{:S(2)}, u32[]{:S(2)}) collective-permute-start(f32[272,512]{1,0:T(8,128)S(1)} %get-tuple-element.264), channel_id=1, source_target_pairs={{0,32},{8,40},{16,48},{24,56},{32,0},{40,8},{48,16},{56,24},{64,96... | collective-permute-start | bytes 1671176 | tf_op jit(solution)/shard_map/ppermute | solution.py:410
  (21 other events, 251.5 us)

commit v4 on v3

--- a/solution.py
+++ b/solution.py
@@ -310,22 +310,19 @@
     rank = mode2.shape[1]
     dot = functools.partial(jnp.dot, preferred_element_type=F32)
 
-    def body(place_ref, col_ref, depth_ref, signs_ref, mode2_ref, mode3_ref, table_ref, x_ref, o_ref, total, gram, held, sems):
+    def body(place_ref, col_ref, depth_ref, signs_ref, mode2_ref, mode3_ref, turn_ref, table_ref, x_ref, o_ref, total, held, sems):
         copies = [pltpu.make_async_copy(x_ref.at[k], held.at[k], sems.at[k]) for k in range(slices)]
         for copy in copies:
             copy.start()
-        total[...] = jnp.zeros((rows, rank), F32)
-        gram[...] = jnp.zeros((rank, rank), F32)
+        total[...] = jnp.zeros((rows + rank, rank), F32)
+        turned = mode2_ref[...].T
 
         for k, copy in enumerate(copies):
             khatri = mode2_ref[...] * mode3_ref[k]
             weighted = khatri * counts(col_ref, depth_ref, k, cols)
-            gram[...] += lax.dot_general(
-                khatri, weighted, (((0,), (0,)), ((), ())), precision=HIGH, preferred_element_type=F32
-            )
             copy.wait()
             weights = jnp.concatenate(in_three(weighted), axis=1)
-            x_high, x_middle, x_low = in_three(held[k])
+            x_high, x_middle, x_low = in_three(jnp.concatenate([held[k], turned * turn_ref[k]], axis=0))
             most = dot(x_high, weights)
             some = dot(x_middle, weights[:, : 2 * rank])
             total[...] += (
@@ -334,19 +331,19 @@
                 + most[:, :rank]
             )
 
-        part = total[...].T * (signs_ref[...] * factor)
+        part = total[:rows].T * (signs_ref[...] * factor)
         done = jnp.zeros((rank, rows), F32)
         for piece in in_three(part):
             done = done + dot(piece, table_ref[...])
         o_ref[:rank] = done
-        square = gram[...]
+        square = total[rows:]
         lines = rank * rank // rows
         o_ref[rank:] = jnp.concatenate([square[q : q + lines] for q in range(0, rank, lines)], axis=1)
 
     return chain(
-        body, (col, depth, signs, mode2, mode3, table, slab), [VMEM] * 6 + [HBM], [struct(rank + rank * rank // rows, rows)], [VMEM],
+        body, (col, depth, signs, mode2, mode3, mode3[:, 0, :, None], table, slab), [VMEM] * 7 + [HBM], [struct(rank + rank * rank // rows, rows)], [VMEM],
         scratch=[
-            pltpu.VMEM((rows, rank), F32), pltpu.VMEM((rank, rank), F32),
+            pltpu.VMEM((rows + rank, rank), F32),
             pltpu.VMEM((slices, rows, cols), F32), pltpu.SemaphoreType.DMA((slices,)),
         ],
         limit=48,

time: 245 us -> 246 us (level)
  no operation moved by 1% of the time
where the time goes in v4:
time: 246 us
  waiting for transfers between devices  116 us (47%)
  Pallas kernels  68.3 us (28%)
  starting transfers between devices  53.5 us (22%)
  local copies, waits for them, and re-layouts  5.96 us (2%)
    ppermute x40, waiting for transfers between devices, swap(): lax.ppermute(value, axis, [(s, s ^ mask) for s in range(lax.axis_size(axi...  116 us
    pallas_call x56, Pallas kernels, __call__(): pl.pallas_call(inner, out_shape=list(out_shapes) + [struct(8, 128)], grid...  68.3 us
    ppermute x40, starting transfers between devices, swap(): lax.ppermute(value, axis, [(s, s ^ mask) for s in range(lax.axis_size(axi...  53.5 us
  transfers between devices with their start and end apart: 40, of which 23 were waited for; matrix products, arithmetic and copies ran while one was open for 0% of the time, Pallas kernels for 23%

profile of v4, /device:TPU:0, one launch (start us, length us, event | category | flops | bytes accessed | tf_op | source)
XLA Modules:
  0.0 246.0 jit_solution(377368144556768221)
XLA Ops:
  6.4 9.5 %shard_map.86 = (f32[72,512]{1,0:T(8,128)S(1)}, f32[8,128]{1,0:T(8,128)S(1)}) custom-call(s32[5]{0:T(128)S(1)} %stack.23.place_ref, s32[1,512]{1,0:T(1,128)S(1)} %bitcast.15, s32[1,512]{1,0:T(1,128)S(1)} %bitcast.16, f32[1,512]{1,0:T(1,128)S(1)} %bitcast.11, f32[512,64]{1,0:T(8,128)S(1)} %copy.15.refs_3_, f32[8,1,64]{2,1,0:T(1,128)S(1)} %bitcast.14, ...), custom_call_target="tpu_custom_call" | custom-call | tf_op jit(solution)/shard_map/pallas_call | solution.py:53
  16.1 5.1 %shard_map.87 = (f32[2,512,512]{2,1,0:T(8,128)S(1)}, f32[2,512,512]{2,1,0:T(8,128)S(1)}, f32[8,128]{1,0:T(8,128)S(1)}) custom-call(s32[5]{0:T(128)S(1)} %stack.23.place_ref, f32[512,1]{1,0:T(8,128)S(1)} %copy.18.refs_0_, bf16[512,512]{1,0:T(8,128)(2,1)S(1)} %copy-done.1, f32[8,512,512]{2,1,0:T(8,128)} %refs_2_.3, f32[8,128]{1,0:T(8,128)S(1)} %get-tuple-element.142.refs_3_), custom_call_target="tpu_custom_call" | custom-call | tf_op jit(solution)/shard_map/pallas_call | solution.py:53
  22.7 5.1 %shard_map.89 = (f32[2,512,512]{2,1,0:T(8,128)S(1)}, f32[2,512,512]{2,1,0:T(8,128)S(1)}, f32[8,128]{1,0:T(8,128)S(1)}) custom-call(s32[5]{0:T(128)S(1)} %stack.23.place_ref, f32[512,1]{1,0:T(8,128)S(1)} %copy.18.refs_0_, bf16[512,512]{1,0:T(8,128)(2,1)S(1)} %copy-done.1, f32[8,512,512]{2,1,0:T(8,128)} %refs_2_.3, f32[8,128]{1,0:T(8,128)S(1)} %get-tuple-element.144.refs_3_), custom_call_target="tpu_custom_call" | custom-call | tf_op jit(solution)/shard_map/pallas_call | solution.py:53
  28.4 3.1 %collective-permute-start.4 = (f32[72,512]{1,0:T(8,128)S(1)}, f32[72,512]{1,0:T(8,128)S(1)}, u32[]{:S(2)}, u32[]{:S(2)}) collective-permute-start(f32[72,512]{1,0:T(8,128)S(1)} %get-tuple-element.148.refs_0_), channel_id=1, source_target_pairs={{0,1},{1,0},{2,3},{3,2},{4,5},{5,4},{6,7},{7,6},{8,9},{9,8},{10,11... | collective-permute-start | bytes 442376 | tf_op jit(solution)/shard_map/ppermute | solution.py:407
  31.5 4.4 %collective-permute-done.4.refs_1_ = f32[72,512]{1,0:T(8,128)S(1)} collective-permute-done((f32[72,512]{1,0:T(8,128)S(1)}, f32[72,512]{1,0:T(8,128)S(1)}, u32[]{:S(2)}, u32[]{:S(2)}) %collective-permute-start.4) | collective-permute-done | bytes 147488 | tf_op jit(solution)/shard_map/ppermute | solution.py:407
  42.5 3.8 %collective-permute-start.11 = (f32[72,512]{1,0:T(8,128)S(1)}, f32[72,512]{1,0:T(8,128)S(1)}, u32[]{:S(2)}, u32[]{:S(2)}) collective-permute-start(f32[72,512]{1,0:T(8,128)S(1)} %get-tuple-element.167.refs_0_), channel_id=1, source_target_pairs={{0,4},{1,5},{2,6},{3,7},{4,0},{5,1},{6,2},{7,3},{8,12},{9,13},{10,... | collective-permute-start | bytes 442376 | tf_op jit(solution)/shard_map/ppermute | solution.py:407
  53.9 2.9 %collective-permute-start.9 = (f32[256,512]{1,0:T(8,128)S(1)}, f32[256,512]{1,0:T(8,128)S(1)}, u32[]{:S(2)}, u32[]{:S(2)}) collective-permute-start(f32[256,512]{1,0:T(8,128)S(1)} %get-tuple-element.162), channel_id=1, source_target_pairs={{0,64},{8,72},{16,80},{24,88},{32,96},{40,104},{48,112},{56,120},{... | collective-permute-start | bytes 1572872 | tf_op jit(solution)/shard_map/ppermute | solution.py:407
  57.7 9.5 %collective-permute-done.8.refs_1_ = f32[256,512]{1,0:T(8,128)S(1)} collective-permute-done((f32[256,512]{1,0:T(8,128)S(1)}, f32[256,512]{1,0:T(8,128)S(1)}, u32[]{:S(2)}, u32[]{:S(2)}) %collective-permute-start.8) | collective-permute-done | bytes 524320 | tf_op jit(solution)/shard_map/ppermute | solution.py:407
  69.5 11.4 %collective-permute-done.9.refs_1_.refs_2_ = f32[256,512]{1,0:T(8,128)S(1)} collective-permute-done((f32[256,512]{1,0:T(8,128)S(1)}, f32[256,512]{1,0:T(8,128)S(1)}, u32[]{:S(2)}, u32[]{:S(2)}) %collective-permute-start.9) | collective-permute-done | bytes 524320 | tf_op jit(solution)/shard_map/ppermute | solution.py:407
  82.9 2.3 collective-permute-start.17
  86.8 5.0 %collective-permute-done.12.refs_1_.refs_3_ = f32[512,512]{1,0:T(8,128)S(1)} collective-permute-done((f32[512,512]{1,0:T(8,128)S(1)}, f32[512,512]{1,0:T(8,128)S(1)}, u32[]{:S(2)}, u32[]{:S(2)}) %collective-permute-start.12) | collective-permute-done | bytes 1048608 | tf_op jit(solution)/shard_map/ppermute | solution.py:407
  97.0 5.0 %collective-permute-done.16.refs_1_.refs_2_ = f32[256,512]{1,0:T(8,128)S(1)} collective-permute-done((f32[256,512]{1,0:T(8,128)S(1)}, f32[256,512]{1,0:T(8,128)S(1)}, u32[]{:S(2)}, u32[]{:S(2)}) %collective-permute-start.16) | collective-permute-done | bytes 524320 | tf_op jit(solution)/shard_map/ppermute | solution.py:407
  108.0 2.7 %collective-permute-done.18.refs_1_ = f32[256,512]{1,0:T(8,128)S(1)} collective-permute-done((f32[256,512]{1,0:T(8,128)S(1)}, f32[256,512]{1,0:T(8,128)S(1)}, u32[]{:S(2)}, u32[]{:S(2)}) %collective-permute-start.18) | collective-permute-done | bytes 524320 | tf_op jit(solution)/shard_map/ppermute | solution.py:407
  113.0 11.4 %collective-permute-done.20.refs_1_.refs_2_ = f32[256,512]{1,0:T(8,128)S(1)} collective-permute-done((f32[256,512]{1,0:T(8,128)S(1)}, f32[256,512]{1,0:T(8,128)S(1)}, u32[]{:S(2)}, u32[]{:S(2)}) %collective-permute-start.20) | collective-permute-done | bytes 524320 | tf_op jit(solution)/shard_map/ppermute | solution.py:407
  129.5 10.5 %collective-permute-done.13.refs_1_.refs_2_ = f32[512,512]{1,0:T(8,128)S(1)} collective-permute-done((f32[512,512]{1,0:T(8,128)S(1)}, f32[512,512]{1,0:T(8,128)S(1)}, u32[]{:S(2)}, u32[]{:S(2)}) %collective-permute-start.13) | collective-permute-done | bytes 1048608 | tf_op jit(solution)/shard_map/ppermute | solution.py:407
  154.2 2.6 %collective-permute-done.24.refs_1_ = f32[256,512]{1,0:T(8,128)S(1)} collective-permute-done((f32[256,512]{1,0:T(8,128)S(1)}, f32[256,512]{1,0:T(8,128)S(1)}, u32[]{:S(2)}, u32[]{:S(2)}) %collective-permute-start.24) | collective-permute-done | bytes 524320 | tf_op jit(solution)/shard_map/ppermute | solution.py:407
  157.5 7.3 %shard_map.123 = (f32[64,64]{1,0:T(8,128)S(1)}, f32[8,128]{1,0:T(8,128)S(1)}) custom-call(s32[5]{0:T(128)S(1)} %stack.23.place_ref, f32[72,512]{1,0:T(8,128)S(1)} %get-tuple-element.169.refs_1_.refs_2_.refs_0_, f32[8,128]{1,0:T(8,128)S(1)} %get-tuple-element.229.refs_1_), custom_call_target="tpu_custom_call" | custom-call | tf_op jit(solution)/shard_map/pallas_call | solution.py:53
  166.4 4.2 %collective-permute-done.26.refs_1_.refs_2_ = f32[256,512]{1,0:T(8,128)S(1)} collective-permute-done((f32[256,512]{1,0:T(8,128)S(1)}, f32[256,512]{1,0:T(8,128)S(1)}, u32[]{:S(2)}, u32[]{:S(2)}) %collective-permute-start.26) | collective-permute-done | bytes 524320 | tf_op jit(solution)/shard_map/ppermute | solution.py:407
  172.6 2.3 collective-permute-start.29
  177.3 16.1 %collective-permute-done.30.refs_1_.refs_3_ = f32[2,256,512]{2,1,0:T(8,128)S(1)} collective-permute-done((f32[2,256,512]{2,1,0:T(8,128)S(1)}, f32[2,256,512]{2,1,0:T(8,128)S(1)}, u32[]{:S(2)}, u32[]{:S(2)}) %collective-permute-start.30) | collective-permute-done | bytes 1048608 | tf_op jit(solution)/shard_map/ppermute | solution.py:407
  204.0 5.8 %collective-permute-done.34.refs_1_ = f32[256,512]{1,0:T(8,128)S(1)} collective-permute-done((f32[256,512]{1,0:T(8,128)S(1)}, f32[256,512]{1,0:T(8,128)S(1)}, u32[]{:S(2)}, u32[]{:S(2)}) %collective-permute-start.34) | collective-permute-done | bytes 524320 | tf_op jit(solution)/shard_map/ppermute | solution.py:407
  211.2 10.4 %collective-permute-done.33.refs_1_.refs_2_ = f32[256,512]{1,0:T(8,128)S(1)} collective-permute-done((f32[256,512]{1,0:T(8,128)S(1)}, f32[256,512]{1,0:T(8,128)S(1)}, u32[]{:S(2)}, u32[]{:S(2)}) %collective-permute-start.33) | collective-permute-done | bytes 524320 | tf_op jit(solution)/shard_map/ppermute | solution.py:407
  229.5 2.8 %collective-permute-done.38.refs_1_ = f32[272,512]{1,0:T(8,128)S(1)} collective-permute-done((f32[272,512]{1,0:T(8,128)S(1)}, f32[272,512]{1,0:T(8,128)S(1)}, u32[]{:S(2)}, u32[]{:S(2)}) %collective-permute-start.38) | collective-permute-done | bytes 557088 | tf_op jit(solution)/shard_map/ppermute | solution.py:407
  234.2 4.3 %collective-permute-done.37.refs_0_.refs_2_ = f32[272,512]{1,0:T(8,128)S(1)} collective-permute-done((f32[272,512]{1,0:T(8,128)S(1)}, f32[272,512]{1,0:T(8,128)S(1)}, u32[]{:S(2)}, u32[]{:S(2)}) %collective-permute-start.37) | collective-permute-done | bytes 557088 | tf_op jit(solution)/shard_map/ppermute | solution.py:407
  (128 shorter events, 97.3 us)
Async XLA Ops:
  28.1 21.2 %collective-permute-start.1 = (f32[2,512,512]{2,1,0:T(8,128)S(1)}, f32[2,512,512]{2,1,0:T(8,128)S(1)}, u32[]{:S(2)}, u32[]{:S(2)}) collective-permute-start(f32[2,512,512]{2,1,0:T(8,128)S(1)} %get-tuple-element.145.refs_0_), channel_id=1, source_target_pairs={{0,8},{8,0},{16,24},{24,16},{32,40},{40,32},{48,56},{56,48},{64,72... | collective-permute-start | bytes 6291464 | tf_op jit(solution)/shard_map/ppermute | solution.py:407
  46.3 39.8 %collective-permute-start.7 = (f32[512,512]{1,0:T(8,128)S(1)}, f32[512,512]{1,0:T(8,128)S(1)}, u32[]{:S(2)}, u32[]{:S(2)}) collective-permute-start(f32[512,512]{1,0:T(8,128)S(1)} %get-tuple-element.159.refs_0_), channel_id=1, source_target_pairs={{0,16},{8,24},{16,0},{24,8},{32,48},{40,56},{48,32},{56,40},{64,80... | collective-permute-start | bytes 3145736 | tf_op jit(solution)/shard_map/ppermute | solution.py:407
  51.4 40.4 %collective-permute-start.12 = (f32[512,512]{1,0:T(8,128)S(1)}, f32[512,512]{1,0:T(8,128)S(1)}, u32[]{:S(2)}, u32[]{:S(2)}) collective-permute-start(f32[512,512]{1,0:T(8,128)S(1)} %get-tuple-element.180.refs_1_), channel_id=1, source_target_pairs={{0,16},{8,24},{16,0},{24,8},{32,48},{40,56},{48,32},{56,40},{64,80... | collective-permute-start | bytes 3145736 | tf_op jit(solution)/shard_map/ppermute | solution.py:407
  53.9 27.0 %collective-permute-start.9 = (f32[256,512]{1,0:T(8,128)S(1)}, f32[256,512]{1,0:T(8,128)S(1)}, u32[]{:S(2)}, u32[]{:S(2)}) collective-permute-start(f32[256,512]{1,0:T(8,128)S(1)} %get-tuple-element.162), channel_id=1, source_target_pairs={{0,64},{8,72},{16,80},{24,88},{32,96},{40,104},{48,112},{56,120},{... | collective-permute-start | bytes 1572872 | tf_op jit(solution)/shard_map/ppermute | solution.py:407
  56.8 25.5 %collective-permute-start.10 = (f32[256,512]{1,0:T(8,128)S(1)}, f32[256,512]{1,0:T(8,128)S(1)}, u32[]{:S(2)}, u32[]{:S(2)}) collective-permute-start(f32[256,512]{1,0:T(8,128)S(1)} %get-tuple-element.163), channel_id=1, source_target_pairs={{0,96},{8,104},{16,112},{24,120},{32,64},{40,72},{48,80},{56,88},{... | collective-permute-start | bytes 1572872 | tf_op jit(solution)/shard_map/ppermute | solution.py:407
  67.8 26.9 %collective-permute-start.15 = (f32[256,512]{1,0:T(8,128)S(1)}, f32[256,512]{1,0:T(8,128)S(1)}, u32[]{:S(2)}, u32[]{:S(2)}) collective-permute-start(f32[256,512]{1,0:T(8,128)S(1)} %get-tuple-element.184), channel_id=1, source_target_pairs={{0,32},{8,40},{16,48},{24,56},{32,0},{40,8},{48,16},{56,24},{64,96... | collective-permute-start | bytes 1572872 | tf_op jit(solution)/shard_map/ppermute | solution.py:407
  92.6 48.1 %collective-permute-start.14 = (f32[576,512]{1,0:T(8,128)S(1)}, f32[576,512]{1,0:T(8,128)S(1)}, u32[]{:S(2)}, u32[]{:S(2)}) collective-permute-start(f32[576,512]{1,0:T(8,128)S(1)} %get-tuple-element.182.refs_1_), channel_id=1, source_target_pairs={{0,16},{8,24},{16,0},{24,8},{32,48},{40,56},{48,32},{56,40},{64,80... | collective-permute-start | bytes 3538952 | tf_op jit(solution)/shard_map/ppermute | solution.py:407
  94.1 45.9 %collective-permute-start.13 = (f32[512,512]{1,0:T(8,128)S(1)}, f32[512,512]{1,0:T(8,128)S(1)}, u32[]{:S(2)}, u32[]{:S(2)}) collective-permute-start(f32[512,512]{1,0:T(8,128)S(1)} %get-tuple-element.178.refs_0_), channel_id=1, source_target_pairs={{0,16},{8,24},{16,0},{24,8},{32,48},{40,56},{48,32},{56,40},{64,80... | collective-permute-start | bytes 3145736 | tf_op jit(solution)/shard_map/ppermute | solution.py:407
  102.6 21.9 %collective-permute-start.20 = (f32[256,512]{1,0:T(8,128)S(1)}, f32[256,512]{1,0:T(8,128)S(1)}, u32[]{:S(2)}, u32[]{:S(2)}) collective-permute-start(f32[256,512]{1,0:T(8,128)S(1)} %get-tuple-element.201), channel_id=1, source_target_pairs={{0,64},{8,72},{16,80},{24,88},{32,96},{40,104},{48,112},{56,120},{... | collective-permute-start | bytes 1572872 | tf_op jit(solution)/shard_map/ppermute | solution.py:407
  104.7 21.5 %collective-permute-start.22 = (f32[256,512]{1,0:T(8,128)S(1)}, f32[256,512]{1,0:T(8,128)S(1)}, u32[]{:S(2)}, u32[]{:S(2)}) collective-permute-start(f32[256,512]{1,0:T(8,128)S(1)} %get-tuple-element.205), channel_id=1, source_target_pairs={{0,96},{8,104},{16,112},{24,120},{32,64},{40,72},{48,80},{56,88},{... | collective-permute-start | bytes 1572872 | tf_op jit(solution)/shard_map/ppermute | solution.py:407
  111.4 29.9 %collective-permute-start.19 = (f32[256,512]{1,0:T(8,128)S(1)}, f32[256,512]{1,0:T(8,128)S(1)}, u32[]{:S(2)}, u32[]{:S(2)}) collective-permute-start(f32[256,512]{1,0:T(8,128)S(1)} %get-tuple-element.199), channel_id=1, source_target_pairs={{0,32},{8,40},{16,48},{24,56},{32,0},{40,8},{48,16},{56,24},{64,96... | collective-permute-start | bytes 1572872 | tf_op jit(solution)/shard_map/ppermute | solution.py:407
  126.8 21.8 %collective-permute-start.23 = (f32[256,512]{1,0:T(8,128)S(1)}, f32[256,512]{1,0:T(8,128)S(1)}, u32[]{:S(2)}, u32[]{:S(2)}) collective-permute-start(f32[256,512]{1,0:T(8,128)S(1)} %get-tuple-element.207), channel_id=1, source_target_pairs={{0,96},{8,104},{16,112},{24,120},{32,64},{40,72},{48,80},{56,88},{... | collective-permute-start | bytes 1572872 | tf_op jit(solution)/shard_map/ppermute | solution.py:407
  146.4 24.2 %collective-permute-start.26 = (f32[256,512]{1,0:T(8,128)S(1)}, f32[256,512]{1,0:T(8,128)S(1)}, u32[]{:S(2)}, u32[]{:S(2)}) collective-permute-start(f32[256,512]{1,0:T(8,128)S(1)} %get-tuple-element.228), channel_id=1, source_target_pairs={{0,64},{8,72},{16,80},{24,88},{32,96},{40,104},{48,112},{56,120},{... | collective-permute-start | bytes 1572872 | tf_op jit(solution)/shard_map/ppermute | solution.py:407
  149.2 22.7 %collective-permute-start.28 = (f32[256,512]{1,0:T(8,128)S(1)}, f32[256,512]{1,0:T(8,128)S(1)}, u32[]{:S(2)}, u32[]{:S(2)}) collective-permute-start(f32[256,512]{1,0:T(8,128)S(1)} %get-tuple-element.233), channel_id=1, source_target_pairs={{0,96},{8,104},{16,112},{24,120},{32,64},{40,72},{48,80},{56,88},{... | collective-permute-start | bytes 1572872 | tf_op jit(solution)/shard_map/ppermute | solution.py:407
  150.6 26.1 %collective-permute-start.31 = (f32[2,256,512]{2,1,0:T(8,128)S(1)}, f32[2,256,512]{2,1,0:T(8,128)S(1)}, u32[]{:S(2)}, u32[]{:S(2)}) collective-permute-start(f32[2,256,512]{2,1,0:T(8,128)S(1)} %get-tuple-element.244.refs_0_), channel_id=1, source_target_pairs={{0,16},{8,24},{16,0},{24,8},{32,48},{40,56},{48,32},{56,40},{64,80... | collective-permute-start | bytes 3145736 | tf_op jit(solution)/shard_map/ppermute | solution.py:407
  152.1 41.3 %collective-permute-start.30 = (f32[2,256,512]{2,1,0:T(8,128)S(1)}, f32[2,256,512]{2,1,0:T(8,128)S(1)}, u32[]{:S(2)}, u32[]{:S(2)}) collective-permute-start(f32[2,256,512]{2,1,0:T(8,128)S(1)} %get-tuple-element.242.refs_1_), channel_id=1, source_target_pairs={{0,16},{8,24},{16,0},{24,8},{32,48},{40,56},{48,32},{56,40},{64,80... | collective-permute-start | bytes 3145736 | tf_op jit(solution)/shard_map/ppermute | solution.py:407
  164.8 29.2 %collective-permute-start.25 = (f32[272,512]{1,0:T(8,128)S(1)}, f32[272,512]{1,0:T(8,128)S(1)}, u32[]{:S(2)}, u32[]{:S(2)}) collective-permute-start(f32[272,512]{1,0:T(8,128)S(1)} %get-tuple-element.226), channel_id=1, source_target_pairs={{0,32},{8,40},{16,48},{24,56},{32,0},{40,8},{48,16},{56,24},{64,96... | collective-permute-start | bytes 1671176 | tf_op jit(solution)/shard_map/ppermute | solution.py:407
  171.2 24.4 %collective-permute-start.27 = (f32[272,512]{1,0:T(8,128)S(1)}, f32[272,512]{1,0:T(8,128)S(1)}, u32[]{:S(2)}, u32[]{:S(2)}) collective-permute-start(f32[272,512]{1,0:T(8,128)S(1)} %get-tuple-element.231), channel_id=1, source_target_pairs={{0,64},{8,72},{16,80},{24,88},{32,96},{40,104},{48,112},{56,120},{... | collective-permute-start | bytes 1671176 | tf_op jit(solution)/shard_map/ppermute | solution.py:407
  172.6 25.6 %collective-permute-start.29 = (f32[272,512]{1,0:T(8,128)S(1)}, f32[272,512]{1,0:T(8,128)S(1)}, u32[]{:S(2)}, u32[]{:S(2)}) collective-permute-start(f32[272,512]{1,0:T(8,128)S(1)} %get-tuple-element.235), channel_id=1, source_target_pairs={{0,96},{8,104},{16,112},{24,120},{32,64},{40,72},{48,80},{56,88},{... | collective-permute-start | bytes 1671176 | tf_op jit(solution)/shard_map/ppermute | solution.py:407
  196.2 25.4 %collective-permute-start.33 = (f32[256,512]{1,0:T(8,128)S(1)}, f32[256,512]{1,0:T(8,128)S(1)}, u32[]{:S(2)}, u32[]{:S(2)}) collective-permute-start(f32[256,512]{1,0:T(8,128)S(1)} %get-tuple-element.254), channel_id=1, source_target_pairs={{0,64},{8,72},{16,80},{24,88},{32,96},{40,104},{48,112},{56,120},{... | collective-permute-start | bytes 1572872 | tf_op jit(solution)/shard_map/ppermute | solution.py:407
  198.8 25.2 %collective-permute-start.32 = (f32[256,512]{1,0:T(8,128)S(1)}, f32[256,512]{1,0:T(8,128)S(1)}, u32[]{:S(2)}, u32[]{:S(2)}) collective-permute-start(f32[256,512]{1,0:T(8,128)S(1)} %get-tuple-element.252), channel_id=1, source_target_pairs={{0,96},{8,104},{16,112},{24,120},{32,64},{40,72},{48,80},{56,88},{... | collective-permute-start | bytes 1572872 | tf_op jit(solution)/shard_map/ppermute | solution.py:407
  201.1 28.4 %collective-permute-start.39 = (f32[2,256,512]{2,1,0:T(8,128)S(1)}, f32[2,256,512]{2,1,0:T(8,128)S(1)}, u32[]{:S(2)}, u32[]{:S(2)}) collective-permute-start(f32[2,256,512]{2,1,0:T(8,128)S(1)} %get-tuple-element.265.refs_2_), channel_id=1, source_target_pairs={{0,16},{8,24},{16,0},{24,8},{32,48},{40,56},{48,32},{56,40},{64,80... | collective-permute-start | bytes 3145736 | tf_op jit(solution)/shard_map/ppermute | solution.py:407
  202.6 39.5 %collective-permute-start.36 = (f32[2,256,512]{2,1,0:T(8,128)S(1)}, f32[2,256,512]{2,1,0:T(8,128)S(1)}, u32[]{:S(2)}, u32[]{:S(2)}) collective-permute-start(f32[2,256,512]{2,1,0:T(8,128)S(1)} %get-tuple-element.261.refs_1_), channel_id=1, source_target_pairs={{0,16},{8,24},{16,0},{24,8},{32,48},{40,56},{48,32},{56,40},{64,80... | collective-permute-start | bytes 3145736 | tf_op jit(solution)/shard_map/ppermute | solution.py:407
  210.4 21.9 %collective-permute-start.38 = (f32[272,512]{1,0:T(8,128)S(1)}, f32[272,512]{1,0:T(8,128)S(1)}, u32[]{:S(2)}, u32[]{:S(2)}) collective-permute-start(f32[272,512]{1,0:T(8,128)S(1)} %get-tuple-element.264), channel_id=1, source_target_pairs={{0,32},{8,40},{16,48},{24,56},{32,0},{40,8},{48,16},{56,24},{64,96... | collective-permute-start | bytes 1671176 | tf_op jit(solution)/shard_map/ppermute | solution.py:407
  (21 other events, 251.8 us)
